TPU v7x, 256 devices: a whole 4x4x8 slice. The times are simulated.
256 devices in a mesh: term: 32 (over z, x_lo, core), sector: 8 (over y, x_hi).
Axes of the slice: x: 4 (x_hi: 2, x_lo: 2; x = x_hi * 2 + x_lo), y: 4, z: 8, core: 2. Of those that a mesh axis runs over, the one named last changes fastest.
Arguments:
- wavefunction: bfloat16 [16, 512, 512], P('sector'), may hold values from -6 to 6
- left_operators: bfloat16 [2048, 512, 512], P(('term', 'sector')), may hold values from -0.25 to 0.25
- right_operators: bfloat16 [2048, 512, 512], P(('term', 'sector')), may hold values from -0.25 to 0.25
- source_sector: int32 [2048], P(('term', 'sector')), may hold values from 0 to 15
- target_sector: int32 [2048], P(('term', 'sector')), may hold values from 0 to 15
- live_terms: int32 [256], P(('term', 'sector')), may hold values from 1 to 8, as said below
- sector_rows: int32 [16], replicated, may hold values from 1 to 512, as said below
Outputs:
- sigma_blocks: float32 [16, 512, 512], P('sector', 'term')
Inputs may be any that keep to these rules, and one draw needn't show every extreme that they name: Term group g = term index * 8 + sector index holds the term slots g * 8 to (g + 1) * 8 - 1; its live slots are the first live_terms[g]; some group has exactly 8. `sector_rows`: some sector uses exactly 512 rows.
All inputs are finite; a program needn't handle non-finite values.
Results may differ from a plain program's by a relative error of at most 0.0029.
Values may be sent and summed in bfloat16 or wider, within the bound.
No kernel may reach another device: no remote copies, remote signals or barrier semaphores. Data moves between devices by JAX's collectives and lax.ppermute only.
A program may use at most 128 MiB of HBM per device.

v0:
```python
import functools

import jax
import jax.numpy as jnp
from jax import lax
from jax.experimental import pallas as pl
from jax.experimental.pallas import tpu as pltpu
from jax.sharding import PartitionSpec as P

UNIT = 32
AXES = ("term", "sector")
DEPTH = 3
SIZES = ((25, 38), (28, 44), (32, 64))


def device_index(x, y, z, core):
    x, y, z = x % 4, y % 4, z % 8
    return (z * 4 + (x % 2) * 2 + core) * 8 + y * 2 + x // 2


def pairs(move):
    every = [(x, y, z, c) for x in range(4) for y in range(4) for z in range(8) for c in range(2)]
    return [(device_index(*at), device_index(*move(*at))) for at in every if move(*at) is not None]


OTHER_CORE = pairs(lambda x, y, z, c: (x, y, z, 1 - c))
FIRST_AXIS = [pairs(lambda x, y, z, c: (x + k * c, y + k * (1 - c), z, c)) for k in range(4)]
ACROSS = (3, 2, 1, 0)
GATHER_FIRST = [
    pairs(lambda x, y, z, c: (x, y + 1, z, c) if c else (ACROSS[x], y, z, c)),
    pairs(lambda x, y, z, c: (x, y + 2, z, c) if c else None),
    pairs(lambda x, y, z, c: (x, y + 3, z, c) if c else None),
]
GATHER_SECOND = [
    pairs(lambda x, y, z, c: (ACROSS[x], y, z, c) if c else (x, y + 1, z, c)),
    pairs(lambda x, y, z, c: (ACROSS[x], y, z, c) if c else (x, y + 2, z, c)),
    pairs(lambda x, y, z, c: None if c else (x, y + 3, z, c)),
]
FROM_CORE_0 = pairs(lambda x, y, z, c: None if c else (x, y, z, 1))
SECOND_AXIS = [pairs(lambda x, y, z, c: (x + k * (1 - c), y + k * c, z, c)) for k in range(4)]


def coordinates():
    term, sector = lax.axis_index("term"), lax.axis_index("sector")
    x_lo, core = lax.rem(lax.div(term, 2), 2), lax.rem(term, 2)
    return 2 * lax.rem(sector, 2) + x_lo, lax.div(sector, 2), lax.div(term, 4), core


def units_of(rows):
    return lax.div(rows + (UNIT - 1), UNIT)


def group_entry(core, place, i):
    along_x = 4 * lax.div(i, 2) + 2 * lax.div(place, 2) + lax.rem(i, 2)
    sector = jnp.where(core == 0, 4 * place + lax.rem(i, 4), along_x)
    first = jnp.where(core == 0, 0, lax.rem(place, 2))
    return sector, first, 1 + core


def group_count(rows_ref, core, place, i):
    sector, first, step = group_entry(core, place, i)
    count = lax.div(units_of(rows_ref[sector]) - first + step - 1, step)
    return jnp.where((core == 0) & (i >= 4), 0, jnp.maximum(count, 0))


def unit_at(u):
    return pl.ds(pl.multiple_of(u * UNIT, UNIT), UNIT)


def choose_kernel(sizes, rows_ref, out_ref):
    units = [units_of(rows_ref[q]) for q in range(16)]
    pair = functools.reduce(jnp.maximum, [units[q] + units[q + 1] for q in range(0, 16, 2)])
    along_y = functools.reduce(jnp.maximum, [sum(units[q : q + 4]) for q in range(0, 16, 4)])
    along_x, across = jnp.int32(0), jnp.int32(0)
    for x_hi in range(2):
        mine = [units[q] for q in range(16) if (q // 2) % 2 == x_hi]
        across = jnp.maximum(across, sum(mine))
        along_x = jnp.maximum(along_x, sum(lax.div(n + 1, 2) for n in mine))
    group = jnp.maximum(jnp.maximum(along_y, along_x), lax.div(across + 1, 2))
    chosen = jnp.int32(len(sizes) - 1)
    for i in reversed(range(len(sizes) - 1)):
        chosen = jnp.where((pair <= sizes[i][0]) & (group <= sizes[i][1]), i, chosen)
    out_ref[0] = chosen


def choose(sector_rows, sizes):
    smem = pl.BlockSpec(memory_space=pltpu.SMEM)
    return pl.pallas_call(
        functools.partial(choose_kernel, sizes),
        out_shape=jax.ShapeDtypeStruct((1,), jnp.int32),
        in_specs=[smem],
        out_specs=smem,
        name="choose",
    )(sector_rows)[0]


def pack_kernel(rows_ref, wave_ref, out_ref):
    core = lax.rem(lax.axis_index("term"), 2)
    sector = lax.axis_index("sector")
    first_units = units_of(rows_ref[2 * sector])
    second_units = units_of(rows_ref[2 * sector + 1])

    def copy_half(half):
        lanes = pl.ds(half * 256, 256)
        for b, units, base in ((0, first_units, 0), (1, second_units, first_units)):

            @pl.loop(0, units)
            def _(u):
                out_ref[unit_at(base + u), :] = wave_ref[b, unit_at(u), lanes]

    for half in range(2):
        pl.when(core == half)(functools.partial(copy_half, half))


def pack_wave(sector_rows, wavefunction, rows):
    vmem = pl.BlockSpec(memory_space=pltpu.VMEM)
    return pl.pallas_call(
        pack_kernel,
        out_shape=jax.ShapeDtypeStruct((rows, 256), jnp.bfloat16),
        in_specs=[pl.BlockSpec(memory_space=pltpu.SMEM), vmem],
        out_specs=vmem,
        compiler_params=pltpu.CompilerParams(vmem_limit_bytes=16 * 1024 * 1024),
        name="pack_wave",
    )(sector_rows, wavefunction)


def join_kernel(rows_ref, own_ref, got1, got2, got3, both_ref, send2_ref, send1_ref):
    x, y, _, core = coordinates()
    x_hi = lax.div(x, 2)
    block_rows = send1_ref.shape[0]

    def one_pair(p, filled):
        pair = jnp.where(core == 0, 2 * y + p, 2 * p + x_hi)
        count = units_of(rows_ref[2 * pair]) + units_of(rows_ref[2 * pair + 1])
        count = jnp.where((core == 0) & (p >= 2), 0, count)
        from_x = jnp.where(p == x_hi, 0, 1)
        k = jnp.where(core == 0, from_x, lax.rem(y - p + 4, 4))
        for source, block in enumerate((own_ref, got1, got2, got3)):

            @pl.loop(0, jnp.where(k == source, count, 0))
            def _(u):
                both_ref[unit_at(filled + u), :] = block[unit_at(u), :]

        return filled + count

    lax.fori_loop(0, 4, one_pair, 0)
    send1_ref[...] = both_ref[:block_rows]

    @pl.when(core == 0)
    def _():
        send2_ref[...] = both_ref[:block_rows]

    @pl.when(core == 1)
    def _():
        send2_ref[...] = both_ref[block_rows:]


def join(sector_rows, own, got, rows):
    vmem = pl.BlockSpec(memory_space=pltpu.VMEM)
    block = jax.ShapeDtypeStruct((rows, 256), jnp.bfloat16)
    return pl.pallas_call(
        join_kernel,
        out_shape=(jax.ShapeDtypeStruct((2 * rows, 256), jnp.bfloat16), block, block),
        in_specs=[pl.BlockSpec(memory_space=pltpu.SMEM)] + [vmem] * 4,
        out_specs=(vmem,) * 3,
        compiler_params=pltpu.CompilerParams(vmem_limit_bytes=24 * 1024 * 1024),
        name="join",
    )(sector_rows, own, *got)


def terms_kernel(
    block_units,
    rows_ref,
    source_ref,
    target_ref,
    live_ref,
    far_source_ref,
    far_target_ref,
    far_live_ref,
    near0,
    near1,
    near2,
    near3,
    far0,
    far1,
    far2,
    far3,
    near_left,
    near_right,
    far_left,
    far_right,
    own_ref,
    send1,
    send2,
    send3,
    acc,
    left_buf,
    right_buf,
    wave_buf,
    half_buf,
    sems,
):
    x, y, _, core = coordinates()
    near_live = live_ref[0]
    total = near_live + far_live_ref[0]

    def facts(i):
        near = i < near_live
        slot = jnp.where(near, i, i - near_live)
        source = jnp.where(near, source_ref[slot], far_source_ref[slot])
        target = jnp.where(near, target_ref[slot], far_target_ref[slot])
        return near, slot, source, target

    def copies(near, slot, buf):
        left = near_left if near else far_left
        right = near_right if near else far_right
        lanes = pl.ds(pl.multiple_of(core * 256, 256), 256)
        return (
            pltpu.make_async_copy(left.at[slot], left_buf.at[buf], sems.at[buf, 0]),
            pltpu.make_async_copy(right.at[slot, lanes], right_buf.at[buf], sems.at[buf, 1]),
        )

    def begin(i):
        near, slot, _, _ = facts(i)
        buf = lax.rem(i, DEPTH)

        @pl.when(near)
        def _():
            for copy in copies(True, slot, buf):
                copy.start()

        @pl.when(jnp.logical_not(near))
        def _():
            for copy in copies(False, slot, buf):
                copy.start()

    for i in range(DEPTH - 1):
        pl.when(i < total)(functools.partial(begin, i))

    for q in range(16):

        @pl.loop(0, units_of(rows_ref[q]))
        def _(u):
            acc[unit_at(q * 16 + u), :] = jnp.zeros((UNIT, 256), jnp.float32)

    def fetch(source, units):
        source_y = lax.div(source, 4)
        pair = lax.div(source, 2)
        odd = lax.rem(source, 2)
        before_odd = jnp.where(odd == 1, units_of(rows_ref[2 * pair]), 0)
        k = lax.rem(y - source_y + 4, 4)
        before = jnp.where(
            lax.rem(pair, 2) == 1, units_of(rows_ref[4 * source_y]) + units_of(rows_ref[4 * source_y + 1]), 0
        )
        in_y = jnp.where(k == 0, 0, k + 1) * block_units + before + before_odd
        source_hi = lax.rem(pair, 2)
        before = before_odd
        for p in range(3):
            both = units_of(rows_ref[4 * p + 2 * source_hi]) + units_of(rows_ref[4 * p + 2 * source_hi + 1])
            before = before + jnp.where(p < source_y, both, 0)
        in_x = jnp.where(source_hi == lax.div(x, 2), 0, 2) * block_units + before
        for memory, layout, half in (
            ((near0, near1, near2, near3), core, core),
            ((far0, far1, far2, far3), 1 - core, 1 - core),
        ):
            first = jnp.where(layout == 0, in_y, in_x)
            low = 0
            for block in memory:
                high = low + block.shape[0] // UNIT
                begin_at, end_at = jnp.maximum(first, low), jnp.minimum(first + units, high)

                @pl.loop(begin_at, end_at)
                def _(u):
                    wave_buf[half, unit_at(u - first), :] = block[unit_at(u - low), :]

                low = high

    def clear_tail(source_rows, depth):
        last = units_of(source_rows) - 1
        keep = last * UNIT + lax.broadcasted_iota(jnp.int32, (UNIT, 256), 0) < source_rows
        for half in range(2):
            tile = wave_buf[half, unit_at(last), :]
            wave_buf[half, unit_at(last), :] = jnp.where(keep, tile, jnp.zeros_like(tile))

            @pl.loop(last + 1, depth // UNIT)
            def _(u):
                wave_buf[half, unit_at(u), :] = jnp.zeros((UNIT, 256), jnp.bfloat16)

    @pl.loop(0, total)
    def _(i):
        pl.when(i + DEPTH - 1 < total)(lambda: begin(i + DEPTH - 1))
        near, slot, source, target = facts(i)
        buf = lax.rem(i, DEPTH)
        source_rows = rows_ref[source]
        target_rows = rows_ref[target]
        fetch(source, units_of(source_rows))
        for copy in copies(True, slot, buf):
            copy.wait()

        def product(depth):
            clear_tail(source_rows, depth)

            @pl.loop(0, lax.div(target_rows + 255, 256))
            def _(part):
                rows = pl.ds(pl.multiple_of(part * 256, 256), 256)
                left = left_buf[buf, rows, pl.ds(0, depth)]
                for half in range(2):
                    wave = wave_buf[half, pl.ds(0, depth), :]
                    product = jnp.dot(left, wave, preferred_element_type=jnp.float32)
                    half_buf[:, half * 256 : half * 256 + 256] = product.astype(jnp.bfloat16)
                out = lax.dot_general(
                    half_buf[...], right_buf[buf], (((1,), (1,)), ((), ())), preferred_element_type=jnp.float32
                )
                acc[pl.ds(pl.multiple_of(target * 512 + part * 256, 256), 256), :] += out

        pl.when(source_rows <= 256)(functools.partial(product, 256))
        pl.when(source_rows > 256)(functools.partial(product, 512))

    place = jnp.where(core == 0, y, x)
    for k, dest in enumerate((own_ref, send1, send2, send3)):
        there = lax.rem(place + k, 4)

        def one_sector(i, filled):
            sector, first, step = group_entry(core, there, i)
            count = group_count(rows_ref, core, there, i)

            @pl.loop(0, count)
            def _(j):
                tile = acc[unit_at(sector * 16 + first + step * j), :]
                dest[unit_at(filled + j), :] = tile.astype(dest.dtype)

            return filled + count

        lax.fori_loop(0, 8, one_sector, 0)


def term_products(rows, small, far_small, near, far, operators, group_rows):
    smem = pl.BlockSpec(memory_space=pltpu.SMEM)
    hbm = pl.BlockSpec(memory_space=pltpu.HBM)
    vmem = pl.BlockSpec(memory_space=pltpu.VMEM)
    send = jax.ShapeDtypeStruct((group_rows, 256), jnp.bfloat16)
    return pl.pallas_call(
        functools.partial(terms_kernel, group_rows // UNIT),
        out_shape=(jax.ShapeDtypeStruct((group_rows, 256), jnp.float32), send, send, send),
        in_specs=[smem] * 7 + [vmem] * 8 + [hbm] * 4,
        out_specs=(vmem,) * 4,
        scratch_shapes=[
            pltpu.VMEM((16 * 512, 256), jnp.float32),
            pltpu.VMEM((DEPTH, 512, 512), jnp.bfloat16),
            pltpu.VMEM((DEPTH, 256, 512), jnp.bfloat16),
            pltpu.VMEM((2, 512, 256), jnp.bfloat16),
            pltpu.VMEM((256, 512), jnp.bfloat16),
            pltpu.SemaphoreType.DMA((DEPTH, 2)),
        ],
        compiler_params=pltpu.CompilerParams(vmem_limit_bytes=30 * 1024 * 1024),
        cost_estimate=pl.CostEstimate(flops=8 * 10**9, bytes_accessed=16 * 2**20, transcendentals=0),
        name="term_products",
    )(rows, *small, *far_small, *near, *far, *operators)


def regroup_kernel(rows_ref, own_ref, got1, got2, got3, keep_ref, send1, send2, send3, blocks):
    x, y, _, core = coordinates()
    place, other = jnp.where(core == 0, y, x), jnp.where(core == 0, x, y)
    blocks[...] = jnp.zeros_like(blocks)

    def one_sector(i, filled):
        _, first, step = group_entry(core, place, i)
        count = group_count(rows_ref, core, place, i)

        @pl.loop(0, count)
        def _(j):
            unit = first + step * j
            at = pl.ds(pl.multiple_of((filled + j) * UNIT, UNIT), UNIT)
            total = own_ref[at, :] + got1[at, :].astype(jnp.float32)
            total = total + got2[at, :].astype(jnp.float32)
            total = total + got3[at, :].astype(jnp.float32)
            there = jnp.where(core == 0, 2 * lax.div(i, 2) + lax.rem(unit, 2), lax.div(i, 2))
            k = lax.rem(there - other + 4, 4)
            to = pl.multiple_of((lax.rem(i, 2) * 8 + lax.div(unit, 2)) * UNIT, UNIT)
            blocks[k, pl.ds(to, UNIT), :] = total

        return filled + count

    lax.fori_loop(0, 8, one_sector, 0)
    keep_ref[...] = blocks[0]
    for k, dest in enumerate((send1, send2, send3)):
        dest[...] = blocks[k + 1].astype(jnp.bfloat16)


def regroup(rows, own, got):
    vmem = pl.BlockSpec(memory_space=pltpu.VMEM)
    send = jax.ShapeDtypeStruct((512, 256), jnp.bfloat16)
    return pl.pallas_call(
        regroup_kernel,
        out_shape=(jax.ShapeDtypeStruct((512, 256), jnp.float32), send, send, send),
        in_specs=[pl.BlockSpec(memory_space=pltpu.SMEM)] + [vmem] * 4,
        out_specs=(vmem,) * 4,
        scratch_shapes=[pltpu.VMEM((4, 512, 256), jnp.float32)],
        compiler_params=pltpu.CompilerParams(vmem_limit_bytes=32 * 1024 * 1024),
        name="regroup",
    )(rows, own, *got)


def spread_kernel(keep_ref, got1, got2, got3, out_ref):
    total = keep_ref[...] + got1[...].astype(jnp.float32)
    total = total + got2[...].astype(jnp.float32)
    total = (total + got3[...].astype(jnp.float32)).astype(jnp.bfloat16)
    for b in range(2):
        for z in range(8):
            start = (b * 8 + z) * UNIT
            out_ref[z, b] = total[start : start + UNIT]


def spread(keep, got):
    vmem = pl.BlockSpec(memory_space=pltpu.VMEM)
    return pl.pallas_call(
        spread_kernel,
        out_shape=jax.ShapeDtypeStruct((8, 2, UNIT, 256), jnp.bfloat16),
        in_specs=[vmem] * 4,
        out_specs=pl.BlockSpec(memory_space=pltpu.VMEM),
        name="spread",
    )(keep, *got)


def add_kernel(parts_ref, keep_ref, send_ref):
    core = lax.rem(lax.axis_index("term"), 2)
    for b in range(2):
        total = parts_ref[0, b].astype(jnp.float32)
        for z in range(1, 8):
            total = total + parts_ref[z, b].astype(jnp.float32)
        low, high = total[:16], total[16:]
        keep_ref[b] = jnp.where(core == 0, low, high)
        send_ref[b] = jnp.where(core == 0, high, low)


def add_parts(parts):
    vmem = pl.BlockSpec(memory_space=pltpu.VMEM)
    half = jax.ShapeDtypeStruct((2, 16, 256), jnp.float32)
    return pl.pallas_call(
        add_kernel, out_shape=(half, half), in_specs=[vmem], out_specs=(vmem, vmem), name="add_parts"
    )(parts)


def finish_kernel(rows_ref, keep_ref, got_ref, out_ref):
    term, sector = lax.axis_index("term"), lax.axis_index("sector")
    core = lax.rem(term, 2)
    row = term * 16 + lax.broadcasted_iota(jnp.int32, (16, 256), 0)
    for b in range(2):
        used = row < rows_ref[2 * sector + b]
        kept = jnp.where(used, keep_ref[b], 0.0)
        got = jnp.where(used, got_ref[b], 0.0)
        out_ref[b, :, :256] = jnp.where(core == 0, kept, got)
        out_ref[b, :, 256:] = jnp.where(core == 0, got, kept)


def finish(rows, keep, got):
    vmem = pl.BlockSpec(memory_space=pltpu.VMEM)
    return pl.pallas_call(
        finish_kernel,
        out_shape=jax.ShapeDtypeStruct((2, 16, 512), jnp.float32),
        in_specs=[pl.BlockSpec(memory_space=pltpu.SMEM), vmem, vmem],
        out_specs=vmem,
        name="finish",
    )(rows, keep, got)


def sized(sizes, wavefunction, left_operators, right_operators, small, sector_rows):
    wave_rows, group_rows = sizes[0] * UNIT, sizes[1] * UNIT
    send = functools.partial(lax.ppermute, axis_name=AXES)
    packed = pack_wave(sector_rows, wavefunction, wave_rows)
    got = [send(packed, perm=perm) for perm in GATHER_FIRST]
    far_small = [send(numbers, perm=OTHER_CORE) for numbers in small]
    far_left = send(left_operators, perm=OTHER_CORE)
    far_right = send(right_operators, perm=OTHER_CORE)
    both, second, first = join(sector_rows, packed, got, group_rows)
    got = [send(block, perm=perm) for block, perm in zip((first, second, first), GATHER_SECOND)]
    near = [both, *got]
    far = [send(block, perm=OTHER_CORE) for block in near[:3]]
    far.append(send(near[3], perm=FROM_CORE_0))
    operators = (left_operators, right_operators, far_left, far_right)
    own, *sends = term_products(sector_rows, small, far_small, near, far, operators, group_rows)
    got = [send(s, perm=FIRST_AXIS[k + 1]) for k, s in enumerate(sends)]
    return regroup(sector_rows, own, got)


def local(
    wavefunction,
    left_operators,
    right_operators,
    source_sector,
    target_sector,
    live_terms,
    sector_rows,
):
    small = (source_sector, target_sector, live_terms)
    branches = [functools.partial(sized, sizes) for sizes in SIZES]
    operands = (wavefunction, left_operators, right_operators, small, sector_rows)
    keep, *sends = lax.switch(choose(sector_rows, SIZES), branches, *operands)
    got = [lax.ppermute(s, AXES, SECOND_AXIS[k + 1]) for k, s in enumerate(sends)]
    parts = spread(keep, got)
    groups = [[z * 4 + place for z in range(8)] for place in range(4)]
    arrived = lax.all_to_all(
        parts, "term", split_axis=0, concat_axis=0, axis_index_groups=groups, tiled=True
    )
    keep, give = add_parts(arrived)
    return finish(sector_rows, keep, lax.ppermute(give, AXES, OTHER_CORE))


def solution(mesh):
    in_specs = (
        P("sector", None, None),
        P(("term", "sector"), None, None),
        P(("term", "sector"), None, None),
        P(("term", "sector")),
        P(("term", "sector")),
        P(("term", "sector")),
        P(),
    )
    out_specs = P("sector", "term", None)
    return jax.shard_map(local, mesh=mesh, in_specs=in_specs, out_specs=out_specs, check_vma=False)
```

profile of v0, /device:TPU:6, one launch (start us, length us, event | category | flops | bytes accessed | tf_op | source)
XLA Modules:
  0.0 125.4 jit_solution(17697607716656159541)
XLA Ops:
  0.0 1.3 %choose.1 = s32[1]{0:T(128)} custom-call(s32[16]{0:T(128)} %rows_ref.3), custom_call_target="tpu_custom_call" | custom-call | tf_op jit(solution)/shard_map/choose/pallas_call | solution.py:88
  1.9 76.2 %conditional.1 = ((f32[512,256]{1,0:T(8,128)S(1)}, bf16[512,256]{1,0:T(8,128)(2,1)S(1)}, bf16[512,256]{1,0:T(8,128)(2,1)S(1)}, bf16[512,256]{1,0:T(8,128)(2,1)S(1)})) conditional(s32[]{:T(128)} %bitcast, (s32[8]{0:T(128)}, s32[8]{0:T(128)}, s32[1]{0:T(128)}, s32[16]{0:T(128)}, bf16[2,512,512]{2,1,0:T(8,128)(2,1)}, ...), branch_computations={%region_0.0_spmd, %region_1.0_spmd, %region_2.0_spmd} | conditional | flops 8000000000 | bytes 102762048 | solution.py:498
  1.9 0.0 copy-start.8
  2.0 0.0 copy-start.11
  2.0 0.0 copy-start.4
  2.0 0.1 collective-permute-start.13
  2.1 0.5 collective-permute-start.14
  2.6 1.3 %pack_wave.3.own_ref = bf16[800,256]{1,0:T(8,128)(2,1)S(1)} custom-call(s32[16]{0:T(128)} %get-tuple-element.47.rows_ref, bf16[2,512,512]{2,1,0:T(8,128)(2,1)} %get-tuple-element.51.wave_ref), custom_call_target="tpu_custom_call" | custom-call | tf_op jit(solution)/shard_map/cond/branch_0_fun/pack_wave/pallas_call | solution.py:117
  3.9 0.7 collective-permute-start.5
  4.6 0.7 collective-permute-start.4
  5.3 2.3 %collective-permute-start.3 = (bf16[800,256]{1,0:T(8,128)(2,1)S(1)}, bf16[800,256]{1,0:T(8,128)(2,1)S(1)}, u32[]{:S(2)}, u32[]{:S(2)}) collective-permute-start(bf16[800,256]{1,0:T(8,128)(2,1)S(1)} %pack_wave.3.own_ref), channel_id=1, source_target_pairs={{0,17},{8,10},{32,49},{40,42},{64,81},{72,74},{96,113},{104,106},{... | collective-permute-start | bytes 1228808 | tf_op jit(solution)/shard_map/cond/branch_0_fun/ppermute | solution.py:471
  7.6 0.0 collective-permute-done.5.got3
  7.6 0.0 collective-permute-done.4.got2
  7.6 6.9 %collective-permute-done.3.got1 = bf16[800,256]{1,0:T(8,128)(2,1)S(1)} collective-permute-done((bf16[800,256]{1,0:T(8,128)(2,1)S(1)}, bf16[800,256]{1,0:T(8,128)(2,1)S(1)}, u32[]{:S(2)}, u32[]{:S(2)}) %collective-permute-start.3) | collective-permute-done | bytes 409632 | tf_op jit(solution)/shard_map/cond/branch_0_fun/ppermute | solution.py:471
  14.5 1.1 join.3
  15.7 3.2 %collective-permute-start.7 = (bf16[1216,256]{1,0:T(8,128)(2,1)S(1)}, bf16[1216,256]{1,0:T(8,128)(2,1)S(1)}, u32[]{:S(2)}, u32[]{:S(2)}) collective-permute-start(bf16[1216,256]{1,0:T(8,128)(2,1)S(1)} %get-tuple-element.54), channel_id=1, source_target_pairs={{0,4},{8,25},{32,36},{40,57},{64,68},{72,89},{96,100},{104,121},{1... | collective-permute-start | bytes 1867784 | tf_op jit(solution)/shard_map/cond/branch_0_fun/ppermute | solution.py:476
  18.9 3.0 %collective-permute-start.8 = (bf16[1216,256]{1,0:T(8,128)(2,1)S(1)}, bf16[1216,256]{1,0:T(8,128)(2,1)S(1)}, u32[]{:S(2)}, u32[]{:S(2)}) collective-permute-start(bf16[1216,256]{1,0:T(8,128)(2,1)S(1)} %get-tuple-element.53), channel_id=1, source_target_pairs={{0,6},{32,38},{64,70},{96,102},{128,134},{160,166},{192,198},{224,... | collective-permute-start | bytes 1867784 | tf_op jit(solution)/shard_map/cond/branch_0_fun/ppermute | solution.py:476
  21.8 6.3 %collective-permute-start.2 = (s32[1]{0:T(128)}, s32[1]{0:T(128)}, u32[]{:S(2)}, u32[]{:S(2)}) collective-permute-start(s32[1]{0:T(128)} %get-tuple-element.50.live_ref), channel_id=1, source_target_pairs={{0,8},{8,0},{32,40},{40,32},{64,72},{72,64},{96,104},{104,96},{128... | collective-permute-start | bytes 20 | tf_op jit(solution)/shard_map/cond/branch_0_fun/ppermute | solution.py:472
  28.2 1.0 collective-permute-done.2.far_live_ref
  29.1 0.0 copy-done.8
  29.1 0.3 collective-permute-start
  29.4 0.8 collective-permute-done.far_source_ref
  30.3 0.0 copy-done.11
  30.3 0.3 collective-permute-start.1
  30.5 0.8 collective-permute-done.1.far_target_ref
  31.4 0.0 collective-permute-start.6
  31.4 0.0 collective-permute-done.7.near2
  31.4 6.6 %collective-permute-start.11 = (bf16[1216,256]{1,0:T(8,128)(2,1)S(1)}, bf16[1216,256]{1,0:T(8,128)(2,1)S(1)}, u32[]{:S(2)}, u32[]{:S(2)}) collective-permute-start(bf16[1216,256]{1,0:T(8,128)(2,1)S(1)} %collective-permute-done.7.near2), channel_id=1, source_target_pairs={{0,8},{8,0},{32,40},{40,32},{64,72},{72,64},{96,104},{104,96},{128... | collective-permute-start | bytes 1867784 | tf_op jit(solution)/shard_map/cond/branch_0_fun/ppermute | solution.py:478
  38.0 0.0 collective-permute-done.8.near3
  38.0 0.0 collective-permute-start.9
  38.0 4.9 %collective-permute-done.6.near1 = bf16[1216,256]{1,0:T(8,128)(2,1)S(1)} collective-permute-done((bf16[1216,256]{1,0:T(8,128)(2,1)S(1)}, bf16[1216,256]{1,0:T(8,128)(2,1)S(1)}, u32[]{:S(2)}, u32[]{:S(2)}) %collective-permute-start.6) | collective-permute-done | bytes 622624 | tf_op jit(solution)/shard_map/cond/branch_0_fun/ppermute | solution.py:476
  42.8 3.4 %collective-permute-start.12 = (bf16[1216,256]{1,0:T(8,128)(2,1)S(1)}, bf16[1216,256]{1,0:T(8,128)(2,1)S(1)}, u32[]{:S(2)}, u32[]{:S(2)}) collective-permute-start(bf16[1216,256]{1,0:T(8,128)(2,1)S(1)} %collective-permute-done.8.near3), channel_id=1, source_target_pairs={{0,8},{32,40},{64,72},{96,104},{128,136},{160,168},{192,200},{224,... | collective-permute-start | bytes 1867784 | tf_op jit(solution)/shard_map/cond/branch_0_fun/ppermute | solution.py:479
  46.3 0.0 collective-permute-done.11.far2
  46.3 0.1 collective-permute-start.10
  46.4 1.5 %collective-permute-done.12.far3 = bf16[1216,256]{1,0:T(8,128)(2,1)S(1)} collective-permute-done((bf16[1216,256]{1,0:T(8,128)(2,1)S(1)}, bf16[1216,256]{1,0:T(8,128)(2,1)S(1)}, u32[]{:S(2)}, u32[]{:S(2)}) %collective-permute-start.12) | collective-permute-done | bytes 622624 | tf_op jit(solution)/shard_map/cond/branch_0_fun/ppermute | solution.py:479
  47.9 0.9 collective-permute-done.10.far1
  48.8 0.0 collective-permute-done.9.far0
  48.8 0.0 collective-permute-done.13.far_left
  48.8 0.0 collective-permute-done.14.far_right
  48.8 8.4 %term_products.3 = (f32[1216,256]{1,0:T(8,128)S(1)}, bf16[1216,256]{1,0:T(8,128)(2,1)S(1)}, bf16[1216,256]{1,0:T(8,128)(2,1)S(1)}, bf16[1216,256]{1,0:T(8,128)(2,1)S(1)}) custom-call(s32[16]{0:T(128)S(1)} %copy-done.4, s32[8]{0:T(128)S(1)} %copy-done.8, s32[8]{0:T(128)S(1)} %copy-done.11, s32[1]{0:T(128)} %get-tuple-element.50.live_ref, ...), custom_call_target="tpu_custom_call" | custom-call | flops 8000000000 | bytes 16777216 | tf_op jit(solution)/shard_map/cond/branch_0_fun/term_products/pallas_call | solution.py:342
  57.2 0.1 collective-permute-start.15
  57.3 1.5 %collective-permute-start.16 = (bf16[1216,256]{1,0:T(8,128)(2,1)S(1)}, bf16[1216,256]{1,0:T(8,128)(2,1)S(1)}, u32[]{:S(2)}, u32[]{:S(2)}) collective-permute-start(bf16[1216,256]{1,0:T(8,128)(2,1)S(1)} %get-tuple-element.59), channel_id=1, source_target_pairs={{0,4},{8,9},{32,36},{40,41},{64,68},{72,73},{96,100},{104,105},{12... | collective-permute-start | bytes 1867784 | tf_op jit(solution)/shard_map/cond/branch_0_fun/ppermute | solution.py:482
  58.8 1.7 %collective-permute-start.17 = (bf16[1216,256]{1,0:T(8,128)(2,1)S(1)}, bf16[1216,256]{1,0:T(8,128)(2,1)S(1)}, u32[]{:S(2)}, u32[]{:S(2)}) collective-permute-start(bf16[1216,256]{1,0:T(8,128)(2,1)S(1)} %get-tuple-element.60), channel_id=1, source_target_pairs={{0,6},{8,25},{32,38},{40,57},{64,70},{72,89},{96,102},{104,121},{1... | collective-permute-start | bytes 1867784 | tf_op jit(solution)/shard_map/cond/branch_0_fun/ppermute | solution.py:482
  60.5 14.9 %collective-permute-done.15.got1 = bf16[1216,256]{1,0:T(8,128)(2,1)S(1)} collective-permute-done((bf16[1216,256]{1,0:T(8,128)(2,1)S(1)}, bf16[1216,256]{1,0:T(8,128)(2,1)S(1)}, u32[]{:S(2)}, u32[]{:S(2)}) %collective-permute-start.15) | collective-permute-done | bytes 622624 | tf_op jit(solution)/shard_map/cond/branch_0_fun/ppermute | solution.py:482
  75.4 0.0 collective-permute-done.16.got2
  75.4 0.9 collective-permute-done.17.got3
  76.3 1.6 %regroup.3 = (f32[512,256]{1,0:T(8,128)S(1)}, bf16[512,256]{1,0:T(8,128)(2,1)S(1)}, bf16[512,256]{1,0:T(8,128)(2,1)S(1)}, bf16[512,256]{1,0:T(8,128)(2,1)S(1)}) custom-call(s32[16]{0:T(128)S(1)} %copy-done.4, f32[1216,256]{1,0:T(8,128)S(1)} %get-tuple-element.57.own_ref, bf16[1216,256]{1,0:T(8,128)(2,1)S(1)} %collective-permute-done.15.got1, ...), custom_call_target="tpu_custom_call" | custom-call | tf_op jit(solution)/shard_map/cond/branch_0_fun/regroup/pallas_call | solution.py:393
  78.1 0.0 copy-start.3
  78.2 0.3 collective-permute-start.54
  78.5 4.9 %collective-permute-start.55 = (bf16[512,256]{1,0:T(8,128)(2,1)S(1)}, bf16[512,256]{1,0:T(8,128)(2,1)S(1)}, u32[]{:S(2)}, u32[]{:S(2)}) collective-permute-start(bf16[512,256]{1,0:T(8,128)(2,1)S(1)} %get-tuple-element.97), channel_id=1, source_target_pairs={{0,1},{8,12},{32,33},{40,44},{64,65},{72,76},{96,97},{104,108},{12... | collective-permute-start | bytes 786440 | tf_op jit(solution)/shard_map/ppermute | solution.py:499
  83.4 1.3 %collective-permute-start.56 = (bf16[512,256]{1,0:T(8,128)(2,1)S(1)}, bf16[512,256]{1,0:T(8,128)(2,1)S(1)}, u32[]{:S(2)}, u32[]{:S(2)}) collective-permute-start(bf16[512,256]{1,0:T(8,128)(2,1)S(1)} %get-tuple-element.98), channel_id=1, source_target_pairs={{0,17},{8,14},{32,49},{40,46},{64,81},{72,78},{96,113},{104,110},{... | collective-permute-start | bytes 786440 | tf_op jit(solution)/shard_map/ppermute | solution.py:499
  84.7 0.0 collective-permute-done.54.got1
  84.7 3.0 %collective-permute-done.55.got2 = bf16[512,256]{1,0:T(8,128)(2,1)S(1)} collective-permute-done((bf16[512,256]{1,0:T(8,128)(2,1)S(1)}, bf16[512,256]{1,0:T(8,128)(2,1)S(1)}, u32[]{:S(2)}, u32[]{:S(2)}) %collective-permute-start.55) | collective-permute-done | bytes 262176 | tf_op jit(solution)/shard_map/ppermute | solution.py:499
  87.7 3.2 %collective-permute-done.56.got3 = bf16[512,256]{1,0:T(8,128)(2,1)S(1)} collective-permute-done((bf16[512,256]{1,0:T(8,128)(2,1)S(1)}, bf16[512,256]{1,0:T(8,128)(2,1)S(1)}, u32[]{:S(2)}, u32[]{:S(2)}) %collective-permute-start.56) | collective-permute-done | bytes 262176 | tf_op jit(solution)/shard_map/ppermute | solution.py:499
  91.0 0.0 copy-done.1
  91.0 0.7 copy-done.2
  91.7 1.9 %spread.1 = bf16[8,2,32,256]{3,2,1,0:T(8,128)(2,1)} custom-call(f32[512,256]{1,0:T(8,128)S(1)} %get-tuple-element.95.keep_ref, bf16[512,256]{1,0:T(8,128)(2,1)} %copy-done, bf16[512,256]{1,0:T(8,128)(2,1)} %copy-done.1, bf16[512,256]{1,0:T(8,128)(2,1)} %copy-done.2), custom_call_target="tpu_custom_call" | custom-call | tf_op jit(solution)/shard_map/spread/pallas_call | solution.py:416
  93.6 26.7 %all_to_all.5.parts_ref = bf16[8,2,32,256]{3,2,1,0:T(8,128)(2,1)} all-to-all(bf16[8,2,32,256]{3,2,1,0:T(8,128)(2,1)} %spread.1), channel_id=1, replica_groups={{0,32,64,96,128,160,192,224},{8,40,72,104,136,168,200,232},{16,48,80,11..., dimensions={0} | all-to-all | bytes 524288 | tf_op jit(solution)/shard_map/all_to_all | solution.py:502
  120.3 1.6 %add_parts.1 = (f32[2,16,256]{2,1,0:T(8,128)}, f32[2,16,256]{2,1,0:T(8,128)}) custom-call(bf16[8,2,32,256]{3,2,1,0:T(8,128)(2,1)} %all_to_all.5.parts_ref), custom_call_target="tpu_custom_call" | custom-call | tf_op jit(solution)/shard_map/add_parts/pallas_call | solution.py:439
  122.0 0.0 collective-permute-start.57
  122.0 1.4 %collective-permute-done.57.got_ref = f32[2,16,256]{2,1,0:T(8,128)S(1)} collective-permute-done((f32[2,16,256]{2,1,0:T(8,128)}, f32[2,16,256]{2,1,0:T(8,128)S(1)}, u32[]{:S(2)}, u32[]{:S(2)}) %collective-permute-start.57) | collective-permute-done | bytes 32800 | tf_op jit(solution)/shard_map/ppermute | solution.py:506
  123.4 0.6 copy-done.7
  124.0 0.0 copy-done.3
  124.0 1.4 %finish.1 = f32[2,16,512]{2,1,0:T(8,128)} custom-call(s32[16]{0:T(128)S(1)} %copy-done.3, f32[2,16,256]{2,1,0:T(8,128)} %get-tuple-element.99.keep_ref, f32[2,16,256]{2,1,0:T(8,128)} %copy-done.7), custom_call_target="tpu_custom_call" | custom-call | tf_op jit(solution)/shard_map/finish/pallas_call | solution.py:458
  (6 shorter events, 0.0 us)
Async XLA Ops:
  1.9 27.2 %copy-start.8 = (s32[8]{0:T(128)S(1)}, s32[8]{0:T(128)}, u32[]{:S(2)}) copy-start(s32[8]{0:T(128)} %get-tuple-element.48.source_ref) | copy-start | bytes 100 | tf_op jit(solution)/shard_map/cond
  2.0 28.3 %copy-start.11 = (s32[8]{0:T(128)S(1)}, s32[8]{0:T(128)}, u32[]{:S(2)}) copy-start(s32[8]{0:T(128)} %get-tuple-element.49.target_ref) | copy-start | bytes 100 | tf_op jit(solution)/shard_map/cond
  2.0 46.8 %copy-start.4 = (s32[16]{0:T(128)S(1)}, s32[16]{0:T(128)}, u32[]{:S(2)}) copy-start(s32[16]{0:T(128)} %get-tuple-element.47.rows_ref) | copy-start | bytes 196 | tf_op jit(solution)/shard_map/cond
  2.0 46.8 %collective-permute-start.13 = (bf16[8,512,512]{2,1,0:T(8,128)(2,1)}, bf16[8,512,512]{2,1,0:T(8,128)(2,1)S(1)}, u32[]{:S(2)}, u32[]{:S(2)}) collective-permute-start(bf16[8,512,512]{2,1,0:T(8,128)(2,1)} %get-tuple-element.55.near_left), channel_id=1, source_target_pairs={{0,8},{8,0},{32,40},{40,32},{64,72},{72,64},{96,104},{104,96},{128... | collective-permute-start | bytes 12582920 | tf_op jit(solution)/shard_map/cond/branch_0_fun/ppermute | solution.py:473
  2.1 46.7 %collective-permute-start.14 = (bf16[8,512,512]{2,1,0:T(8,128)(2,1)}, bf16[8,512,512]{2,1,0:T(8,128)(2,1)S(1)}, u32[]{:S(2)}, u32[]{:S(2)}) collective-permute-start(bf16[8,512,512]{2,1,0:T(8,128)(2,1)} %get-tuple-element.56.near_right), channel_id=1, source_target_pairs={{0,8},{8,0},{32,40},{40,32},{64,72},{72,64},{96,104},{104,96},{128... | collective-permute-start | bytes 12582920 | tf_op jit(solution)/shard_map/cond/branch_0_fun/ppermute | solution.py:474
  3.9 3.7 %collective-permute-start.5 = (bf16[800,256]{1,0:T(8,128)(2,1)S(1)}, bf16[800,256]{1,0:T(8,128)(2,1)S(1)}, u32[]{:S(2)}, u32[]{:S(2)}) collective-permute-start(bf16[800,256]{1,0:T(8,128)(2,1)S(1)} %pack_wave.3.own_ref), channel_id=1, source_target_pairs={{8,14},{40,46},{72,78},{104,110},{136,142},{168,174},{200,206},{23... | collective-permute-start | bytes 1228808 | tf_op jit(solution)/shard_map/cond/branch_0_fun/ppermute | solution.py:471
  4.6 3.0 %collective-permute-start.4 = (bf16[800,256]{1,0:T(8,128)(2,1)S(1)}, bf16[800,256]{1,0:T(8,128)(2,1)S(1)}, u32[]{:S(2)}, u32[]{:S(2)}) collective-permute-start(bf16[800,256]{1,0:T(8,128)(2,1)S(1)} %pack_wave.3.own_ref), channel_id=1, source_target_pairs={{8,12},{40,44},{72,76},{104,108},{136,140},{168,172},{200,204},{23... | collective-permute-start | bytes 1228808 | tf_op jit(solution)/shard_map/cond/branch_0_fun/ppermute | solution.py:471
  5.3 9.2 %collective-permute-start.3 = (bf16[800,256]{1,0:T(8,128)(2,1)S(1)}, bf16[800,256]{1,0:T(8,128)(2,1)S(1)}, u32[]{:S(2)}, u32[]{:S(2)}) collective-permute-start(bf16[800,256]{1,0:T(8,128)(2,1)S(1)} %pack_wave.3.own_ref), channel_id=1, source_target_pairs={{0,17},{8,10},{32,49},{40,42},{64,81},{72,74},{96,113},{104,106},{... | collective-permute-start | bytes 1228808 | tf_op jit(solution)/shard_map/cond/branch_0_fun/ppermute | solution.py:471
  15.7 15.7 %collective-permute-start.7 = (bf16[1216,256]{1,0:T(8,128)(2,1)S(1)}, bf16[1216,256]{1,0:T(8,128)(2,1)S(1)}, u32[]{:S(2)}, u32[]{:S(2)}) collective-permute-start(bf16[1216,256]{1,0:T(8,128)(2,1)S(1)} %get-tuple-element.54), channel_id=1, source_target_pairs={{0,4},{8,25},{32,36},{40,57},{64,68},{72,89},{96,100},{104,121},{1... | collective-permute-start | bytes 1867784 | tf_op jit(solution)/shard_map/cond/branch_0_fun/ppermute | solution.py:476
  18.9 19.1 %collective-permute-start.8 = (bf16[1216,256]{1,0:T(8,128)(2,1)S(1)}, bf16[1216,256]{1,0:T(8,128)(2,1)S(1)}, u32[]{:S(2)}, u32[]{:S(2)}) collective-permute-start(bf16[1216,256]{1,0:T(8,128)(2,1)S(1)} %get-tuple-element.53), channel_id=1, source_target_pairs={{0,6},{32,38},{64,70},{96,102},{128,134},{160,166},{192,198},{224,... | collective-permute-start | bytes 1867784 | tf_op jit(solution)/shard_map/cond/branch_0_fun/ppermute | solution.py:476
  21.8 7.3 %collective-permute-start.2 = (s32[1]{0:T(128)}, s32[1]{0:T(128)}, u32[]{:S(2)}, u32[]{:S(2)}) collective-permute-start(s32[1]{0:T(128)} %get-tuple-element.50.live_ref), channel_id=1, source_target_pairs={{0,8},{8,0},{32,40},{40,32},{64,72},{72,64},{96,104},{104,96},{128... | collective-permute-start | bytes 20 | tf_op jit(solution)/shard_map/cond/branch_0_fun/ppermute | solution.py:472
  29.1 1.1 collective-permute-start
  30.3 1.1 collective-permute-start.1
  31.4 11.4 %collective-permute-start.6 = (bf16[1216,256]{1,0:T(8,128)(2,1)S(1)}, bf16[1216,256]{1,0:T(8,128)(2,1)S(1)}, u32[]{:S(2)}, u32[]{:S(2)}) collective-permute-start(bf16[1216,256]{1,0:T(8,128)(2,1)S(1)} %get-tuple-element.53), channel_id=1, source_target_pairs={{0,2},{8,25},{32,34},{40,57},{64,66},{72,89},{96,98},{104,121},{12... | collective-permute-start | bytes 1867784 | tf_op jit(solution)/shard_map/cond/branch_0_fun/ppermute | solution.py:476
  31.4 14.9 %collective-permute-start.11 = (bf16[1216,256]{1,0:T(8,128)(2,1)S(1)}, bf16[1216,256]{1,0:T(8,128)(2,1)S(1)}, u32[]{:S(2)}, u32[]{:S(2)}) collective-permute-start(bf16[1216,256]{1,0:T(8,128)(2,1)S(1)} %collective-permute-done.7.near2), channel_id=1, source_target_pairs={{0,8},{8,0},{32,40},{40,32},{64,72},{72,64},{96,104},{104,96},{128... | collective-permute-start | bytes 1867784 | tf_op jit(solution)/shard_map/cond/branch_0_fun/ppermute | solution.py:478
  38.0 10.8 %collective-permute-start.9 = (bf16[2432,256]{1,0:T(8,128)(2,1)S(1)}, bf16[2432,256]{1,0:T(8,128)(2,1)S(1)}, u32[]{:S(2)}, u32[]{:S(2)}) collective-permute-start(bf16[2432,256]{1,0:T(8,128)(2,1)S(1)} %get-tuple-element.52.near0), channel_id=1, source_target_pairs={{0,8},{8,0},{32,40},{40,32},{64,72},{72,64},{96,104},{104,96},{128... | collective-permute-start | bytes 3735560 | tf_op jit(solution)/shard_map/cond/branch_0_fun/ppermute | solution.py:478
  42.8 5.1 %collective-permute-start.12 = (bf16[1216,256]{1,0:T(8,128)(2,1)S(1)}, bf16[1216,256]{1,0:T(8,128)(2,1)S(1)}, u32[]{:S(2)}, u32[]{:S(2)}) collective-permute-start(bf16[1216,256]{1,0:T(8,128)(2,1)S(1)} %collective-permute-done.8.near3), channel_id=1, source_target_pairs={{0,8},{32,40},{64,72},{96,104},{128,136},{160,168},{192,200},{224,... | collective-permute-start | bytes 1867784 | tf_op jit(solution)/shard_map/cond/branch_0_fun/ppermute | solution.py:479
  46.3 2.5 %collective-permute-start.10 = (bf16[1216,256]{1,0:T(8,128)(2,1)S(1)}, bf16[1216,256]{1,0:T(8,128)(2,1)S(1)}, u32[]{:S(2)}, u32[]{:S(2)}) collective-permute-start(bf16[1216,256]{1,0:T(8,128)(2,1)S(1)} %collective-permute-done.6.near1), channel_id=1, source_target_pairs={{0,8},{8,0},{32,40},{40,32},{64,72},{72,64},{96,104},{104,96},{128... | collective-permute-start | bytes 1867784 | tf_op jit(solution)/shard_map/cond/branch_0_fun/ppermute | solution.py:478
  57.2 18.2 %collective-permute-start.15 = (bf16[1216,256]{1,0:T(8,128)(2,1)S(1)}, bf16[1216,256]{1,0:T(8,128)(2,1)S(1)}, u32[]{:S(2)}, u32[]{:S(2)}) collective-permute-start(bf16[1216,256]{1,0:T(8,128)(2,1)S(1)} %get-tuple-element.58), channel_id=1, source_target_pairs={{0,2},{8,24},{32,34},{40,56},{64,66},{72,88},{96,98},{104,120},{12... | collective-permute-start | bytes 1867784 | tf_op jit(solution)/shard_map/cond/branch_0_fun/ppermute | solution.py:482
  57.3 18.1 %collective-permute-start.16 = (bf16[1216,256]{1,0:T(8,128)(2,1)S(1)}, bf16[1216,256]{1,0:T(8,128)(2,1)S(1)}, u32[]{:S(2)}, u32[]{:S(2)}) collective-permute-start(bf16[1216,256]{1,0:T(8,128)(2,1)S(1)} %get-tuple-element.59), channel_id=1, source_target_pairs={{0,4},{8,9},{32,36},{40,41},{64,68},{72,73},{96,100},{104,105},{12... | collective-permute-start | bytes 1867784 | tf_op jit(solution)/shard_map/cond/branch_0_fun/ppermute | solution.py:482
  58.8 17.5 %collective-permute-start.17 = (bf16[1216,256]{1,0:T(8,128)(2,1)S(1)}, bf16[1216,256]{1,0:T(8,128)(2,1)S(1)}, u32[]{:S(2)}, u32[]{:S(2)}) collective-permute-start(bf16[1216,256]{1,0:T(8,128)(2,1)S(1)} %get-tuple-element.60), channel_id=1, source_target_pairs={{0,6},{8,25},{32,38},{40,57},{64,70},{72,89},{96,102},{104,121},{1... | collective-permute-start | bytes 1867784 | tf_op jit(solution)/shard_map/cond/branch_0_fun/ppermute | solution.py:482
  78.1 45.8 %copy-start.3 = (s32[16]{0:T(128)S(1)}, s32[16]{0:T(128)}, u32[]{:S(2)}) copy-start(s32[16]{0:T(128)} %rows_ref.3) | copy-start | bytes 196
  78.2 6.6 %collective-permute-start.54 = (bf16[512,256]{1,0:T(8,128)(2,1)S(1)}, bf16[512,256]{1,0:T(8,128)(2,1)S(1)}, u32[]{:S(2)}, u32[]{:S(2)}) collective-permute-start(bf16[512,256]{1,0:T(8,128)(2,1)S(1)} %get-tuple-element.96), channel_id=1, source_target_pairs={{0,16},{8,10},{32,48},{40,42},{64,80},{72,74},{96,112},{104,106},{... | collective-permute-start | bytes 786440 | tf_op jit(solution)/shard_map/ppermute | solution.py:499
  78.5 9.3 %collective-permute-start.55 = (bf16[512,256]{1,0:T(8,128)(2,1)S(1)}, bf16[512,256]{1,0:T(8,128)(2,1)S(1)}, u32[]{:S(2)}, u32[]{:S(2)}) collective-permute-start(bf16[512,256]{1,0:T(8,128)(2,1)S(1)} %get-tuple-element.97), channel_id=1, source_target_pairs={{0,1},{8,12},{32,33},{40,44},{64,65},{72,76},{96,97},{104,108},{12... | collective-permute-start | bytes 786440 | tf_op jit(solution)/shard_map/ppermute | solution.py:499
  83.4 7.6 %collective-permute-start.56 = (bf16[512,256]{1,0:T(8,128)(2,1)S(1)}, bf16[512,256]{1,0:T(8,128)(2,1)S(1)}, u32[]{:S(2)}, u32[]{:S(2)}) collective-permute-start(bf16[512,256]{1,0:T(8,128)(2,1)S(1)} %get-tuple-element.98), channel_id=1, source_target_pairs={{0,17},{8,14},{32,49},{40,46},{64,81},{72,78},{96,113},{104,110},{... | collective-permute-start | bytes 786440 | tf_op jit(solution)/shard_map/ppermute | solution.py:499
  84.7 6.3 %copy-start = (bf16[512,256]{1,0:T(8,128)(2,1)}, bf16[512,256]{1,0:T(8,128)(2,1)S(1)}, u32[]{:S(2)}) copy-start(bf16[512,256]{1,0:T(8,128)(2,1)S(1)} %collective-permute-done.54.got1) | copy-start | bytes 786436
  87.7 3.2 %copy-start.1 = (bf16[512,256]{1,0:T(8,128)(2,1)}, bf16[512,256]{1,0:T(8,128)(2,1)S(1)}, u32[]{:S(2)}) copy-start(bf16[512,256]{1,0:T(8,128)(2,1)S(1)} %collective-permute-done.55.got2) | copy-start | bytes 786436
  91.0 0.7 copy-start.2
  122.0 1.4 %collective-permute-start.57 = (f32[2,16,256]{2,1,0:T(8,128)}, f32[2,16,256]{2,1,0:T(8,128)S(1)}, u32[]{:S(2)}, u32[]{:S(2)}) collective-permute-start(f32[2,16,256]{2,1,0:T(8,128)} %get-tuple-element.100), channel_id=1, source_target_pairs={{0,8},{8,0},{32,40},{40,32},{64,72},{72,64},{96,104},{104,96},{128... | collective-permute-start | bytes 98312 | tf_op jit(solution)/shard_map/ppermute | solution.py:506
  123.4 0.6 copy-start.7
where the time goes:
time: 128 us; the launch traced here: 125 us
  waiting for transfers between devices  40.3 us (31%)
  starting transfers between devices  37.3 us (29%)
  blocking collectives  26.7 us (21%)
  Pallas kernels  18.7 us (15%)
  local copies, waits for them, and re-layouts  1.36 us (1%)
    all_to_all x1, blocking collectives, local(): lax.all_to_all(parts, 'term', split_axis=0, concat_axis=0, axis_index_gro...  26.7 us
    ppermute x3, waiting for transfers between devices, sized(): got = [send(s, perm=FIRST_AXIS[k + 1]) for k, s in enumerate(sends)]  15.8 us
    pallas_call x1, Pallas kernels, term_products(): pl.pallas_call(functools.partial(terms_kernel, group_rows // UNIT), out_s...  8.38 us
    ppermute x3, waiting for transfers between devices, sized(): got = [send(packed, perm=perm) for perm in GATHER_FIRST]  6.91 us
    ppermute x3, starting transfers between devices, sized(): far_small = [send(numbers, perm=OTHER_CORE) for numbers in small]  6.9 us
    ppermute x3, starting transfers between devices, sized(): far = [send(block, perm=OTHER_CORE) for block in near[:3]]  6.67 us
    ppermute x3, starting transfers between devices, local(): lax.ppermute(s, AXES, SECOND_AXIS[k + 1])  6.55 us
    ppermute x3, waiting for transfers between devices, local(): lax.ppermute(s, AXES, SECOND_AXIS[k + 1])  6.26 us
  transfers between devices with their start and end apart: 22, of which 12 were waited for; matrix products, arithmetic and copies ran while one was open for 0% of the time, Pallas kernels for 2%

commit v1 on v0

--- a/solution.py
+++ b/solution.py
@@ -8,6 +8,7 @@
 from jax.sharding import PartitionSpec as P
 
 UNIT = 32
+TILE = 16
 AXES = ("term", "sector")
 DEPTH = 3
 SIZES = ((25, 38), (28, 44), (32, 64))
@@ -65,6 +66,10 @@
 
 def unit_at(u):
     return pl.ds(pl.multiple_of(u * UNIT, UNIT), UNIT)
+
+
+def tile_at(u):
+    return pl.ds(pl.multiple_of(u * TILE, TILE), TILE)
 
 
 def choose_kernel(sizes, rows_ref, out_ref):
@@ -197,7 +202,6 @@
     left_buf,
     right_buf,
     wave_buf,
-    half_buf,
     sems,
 ):
     x, y, _, core = coordinates()
@@ -214,10 +218,9 @@
     def copies(near, slot, buf):
         left = near_left if near else far_left
         right = near_right if near else far_right
-        lanes = pl.ds(pl.multiple_of(core * 256, 256), 256)
         return (
-            pltpu.make_async_copy(left.at[slot], left_buf.at[buf], sems.at[buf, 0]),
-            pltpu.make_async_copy(right.at[slot, lanes], right_buf.at[buf], sems.at[buf, 1]),
+            pltpu.make_async_copy(left.at[slot, :, core], left_buf.at[buf], sems.at[buf, 0]),
+            pltpu.make_async_copy(right.at[slot], right_buf.at[buf], sems.at[buf, 1]),
         )
 
     def begin(i):
@@ -241,7 +244,7 @@
 
         @pl.loop(0, units_of(rows_ref[q]))
         def _(u):
-            acc[unit_at(q * 16 + u), :] = jnp.zeros((UNIT, 256), jnp.float32)
+            acc[tile_at(q * 16 + u), :] = jnp.zeros((TILE, 512), jnp.float32)
 
     def fetch(source, units):
         source_y = lax.div(source, 4)
@@ -297,24 +300,27 @@
         for copy in copies(True, slot, buf):
             copy.wait()
 
-        def product(depth):
-            clear_tail(source_rows, depth)
-
-            @pl.loop(0, lax.div(target_rows + 255, 256))
-            def _(part):
-                rows = pl.ds(pl.multiple_of(part * 256, 256), 256)
-                left = left_buf[buf, rows, pl.ds(0, depth)]
-                for half in range(2):
-                    wave = wave_buf[half, pl.ds(0, depth), :]
-                    product = jnp.dot(left, wave, preferred_element_type=jnp.float32)
-                    half_buf[:, half * 256 : half * 256 + 256] = product.astype(jnp.bfloat16)
-                out = lax.dot_general(
-                    half_buf[...], right_buf[buf], (((1,), (1,)), ((), ())), preferred_element_type=jnp.float32
-                )
-                acc[pl.ds(pl.multiple_of(target * 512 + part * 256, 256), 256), :] += out
-
-        pl.when(source_rows <= 256)(functools.partial(product, 256))
-        pl.when(source_rows > 256)(functools.partial(product, 512))
+        def product(tiles, depth):
+            left = left_buf[buf, pl.ds(0, tiles), :, pl.ds(0, depth)].reshape(tiles * TILE, depth)
+            halves = []
+            for half in range(2):
+                part = jnp.dot(left, wave_buf[half, pl.ds(0, depth), :], preferred_element_type=jnp.float32)
+                halves.append(part.astype(jnp.bfloat16))
+            out = lax.dot_general(
+                jnp.concatenate(halves, axis=1),
+                right_buf[buf],
+                (((1,), (1,)), ((), ())),
+                preferred_element_type=jnp.float32,
+            )
+            acc[pl.ds(pl.multiple_of(target * 256, 256), tiles * TILE), :] += out
+
+        for depth in (256, 512):
+
+            @pl.when((source_rows <= 256) if depth == 256 else (source_rows > 256))
+            def _():
+                clear_tail(source_rows, depth)
+                pl.when(target_rows <= 256)(functools.partial(product, 8, depth))
+                pl.when(target_rows > 256)(functools.partial(product, 16, depth))
 
     place = jnp.where(core == 0, y, x)
     for k, dest in enumerate((own_ref, send1, send2, send3)):
@@ -326,30 +332,29 @@
 
             @pl.loop(0, count)
             def _(j):
-                tile = acc[unit_at(sector * 16 + first + step * j), :]
-                dest[unit_at(filled + j), :] = tile.astype(dest.dtype)
+                tile = acc[tile_at(sector * 16 + first + step * j), :]
+                dest[tile_at(filled + j), :] = tile.astype(dest.dtype)
 
             return filled + count
 
         lax.fori_loop(0, 8, one_sector, 0)
 
 
-def term_products(rows, small, far_small, near, far, operators, group_rows):
+def term_products(rows, small, far_small, near, far, operators, group_units):
     smem = pl.BlockSpec(memory_space=pltpu.SMEM)
     hbm = pl.BlockSpec(memory_space=pltpu.HBM)
     vmem = pl.BlockSpec(memory_space=pltpu.VMEM)
-    send = jax.ShapeDtypeStruct((group_rows, 256), jnp.bfloat16)
-    return pl.pallas_call(
-        functools.partial(terms_kernel, group_rows // UNIT),
-        out_shape=(jax.ShapeDtypeStruct((group_rows, 256), jnp.float32), send, send, send),
+    send = jax.ShapeDtypeStruct((group_units * TILE, 512), jnp.bfloat16)
+    return pl.pallas_call(
+        functools.partial(terms_kernel, group_units),
+        out_shape=(jax.ShapeDtypeStruct((group_units * TILE, 512), jnp.float32), send, send, send),
         in_specs=[smem] * 7 + [vmem] * 8 + [hbm] * 4,
         out_specs=(vmem,) * 4,
         scratch_shapes=[
-            pltpu.VMEM((16 * 512, 256), jnp.float32),
+            pltpu.VMEM((16 * 256, 512), jnp.float32),
+            pltpu.VMEM((DEPTH, 16, TILE, 512), jnp.bfloat16),
             pltpu.VMEM((DEPTH, 512, 512), jnp.bfloat16),
-            pltpu.VMEM((DEPTH, 256, 512), jnp.bfloat16),
             pltpu.VMEM((2, 512, 256), jnp.bfloat16),
-            pltpu.VMEM((256, 512), jnp.bfloat16),
             pltpu.SemaphoreType.DMA((DEPTH, 2)),
         ],
         compiler_params=pltpu.CompilerParams(vmem_limit_bytes=30 * 1024 * 1024),
@@ -370,14 +375,13 @@
         @pl.loop(0, count)
         def _(j):
             unit = first + step * j
-            at = pl.ds(pl.multiple_of((filled + j) * UNIT, UNIT), UNIT)
+            at = tile_at(filled + j)
             total = own_ref[at, :] + got1[at, :].astype(jnp.float32)
             total = total + got2[at, :].astype(jnp.float32)
             total = total + got3[at, :].astype(jnp.float32)
             there = jnp.where(core == 0, 2 * lax.div(i, 2) + lax.rem(unit, 2), lax.div(i, 2))
             k = lax.rem(there - other + 4, 4)
-            to = pl.multiple_of((lax.rem(i, 2) * 8 + lax.div(unit, 2)) * UNIT, UNIT)
-            blocks[k, pl.ds(to, UNIT), :] = total
+            blocks[k, tile_at(lax.rem(i, 2) * 8 + lax.div(unit, 2)), :] = total
 
         return filled + count
 
@@ -389,87 +393,65 @@
 
 def regroup(rows, own, got):
     vmem = pl.BlockSpec(memory_space=pltpu.VMEM)
-    send = jax.ShapeDtypeStruct((512, 256), jnp.bfloat16)
+    send = jax.ShapeDtypeStruct((256, 512), jnp.bfloat16)
     return pl.pallas_call(
         regroup_kernel,
-        out_shape=(jax.ShapeDtypeStruct((512, 256), jnp.float32), send, send, send),
+        out_shape=(jax.ShapeDtypeStruct((256, 512), jnp.float32), send, send, send),
         in_specs=[pl.BlockSpec(memory_space=pltpu.SMEM)] + [vmem] * 4,
         out_specs=(vmem,) * 4,
-        scratch_shapes=[pltpu.VMEM((4, 512, 256), jnp.float32)],
-        compiler_params=pltpu.CompilerParams(vmem_limit_bytes=32 * 1024 * 1024),
+        scratch_shapes=[pltpu.VMEM((4, 256, 512), jnp.float32)],
+        compiler_params=pltpu.CompilerParams(vmem_limit_bytes=24 * 1024 * 1024),
         name="regroup",
     )(rows, own, *got)
 
 
 def spread_kernel(keep_ref, got1, got2, got3, out_ref):
-    total = keep_ref[...] + got1[...].astype(jnp.float32)
-    total = total + got2[...].astype(jnp.float32)
-    total = (total + got3[...].astype(jnp.float32)).astype(jnp.bfloat16)
     for b in range(2):
         for z in range(8):
-            start = (b * 8 + z) * UNIT
-            out_ref[z, b] = total[start : start + UNIT]
+            at = pl.ds((b * 8 + z) * TILE, TILE)
+            total = keep_ref[at, :] + got1[at, :].astype(jnp.float32)
+            total = total + got2[at, :].astype(jnp.float32)
+            total = total + got3[at, :].astype(jnp.float32)
+            out_ref[z, b] = total.astype(jnp.bfloat16)
 
 
 def spread(keep, got):
     vmem = pl.BlockSpec(memory_space=pltpu.VMEM)
     return pl.pallas_call(
         spread_kernel,
-        out_shape=jax.ShapeDtypeStruct((8, 2, UNIT, 256), jnp.bfloat16),
+        out_shape=jax.ShapeDtypeStruct((8, 2, TILE, 512), jnp.bfloat16),
         in_specs=[vmem] * 4,
-        out_specs=pl.BlockSpec(memory_space=pltpu.VMEM),
+        out_specs=vmem,
         name="spread",
     )(keep, *got)
 
 
-def add_kernel(parts_ref, keep_ref, send_ref):
-    core = lax.rem(lax.axis_index("term"), 2)
+def finish_kernel(rows_ref, parts_ref, out_ref):
+    term, sector = lax.axis_index("term"), lax.axis_index("sector")
+    row = term * TILE + lax.broadcasted_iota(jnp.int32, (TILE, 512), 0)
     for b in range(2):
         total = parts_ref[0, b].astype(jnp.float32)
         for z in range(1, 8):
             total = total + parts_ref[z, b].astype(jnp.float32)
-        low, high = total[:16], total[16:]
-        keep_ref[b] = jnp.where(core == 0, low, high)
-        send_ref[b] = jnp.where(core == 0, high, low)
-
-
-def add_parts(parts):
+        out_ref[b] = jnp.where(row < rows_ref[2 * sector + b], total, 0.0)
+
+
+def finish(rows, parts):
     vmem = pl.BlockSpec(memory_space=pltpu.VMEM)
-    half = jax.ShapeDtypeStruct((2, 16, 256), jnp.float32)
-    return pl.pallas_call(
-        add_kernel, out_shape=(half, half), in_specs=[vmem], out_specs=(vmem, vmem), name="add_parts"
-    )(parts)
-
-
-def finish_kernel(rows_ref, keep_ref, got_ref, out_ref):
-    term, sector = lax.axis_index("term"), lax.axis_index("sector")
-    core = lax.rem(term, 2)
-    row = term * 16 + lax.broadcasted_iota(jnp.int32, (16, 256), 0)
-    for b in range(2):
-        used = row < rows_ref[2 * sector + b]
-        kept = jnp.where(used, keep_ref[b], 0.0)
-        got = jnp.where(used, got_ref[b], 0.0)
-        out_ref[b, :, :256] = jnp.where(core == 0, kept, got)
-        out_ref[b, :, 256:] = jnp.where(core == 0, got, kept)
-
-
-def finish(rows, keep, got):
-    vmem = pl.BlockSpec(memory_space=pltpu.VMEM)
     return pl.pallas_call(
         finish_kernel,
-        out_shape=jax.ShapeDtypeStruct((2, 16, 512), jnp.float32),
-        in_specs=[pl.BlockSpec(memory_space=pltpu.SMEM), vmem, vmem],
+        out_shape=jax.ShapeDtypeStruct((2, TILE, 512), jnp.float32),
+        in_specs=[pl.BlockSpec(memory_space=pltpu.SMEM), vmem],
         out_specs=vmem,
         name="finish",
-    )(rows, keep, got)
-
-
-def sized(sizes, wavefunction, left_operators, right_operators, small, sector_rows):
+    )(rows, parts)
+
+
+def sized(sizes, wavefunction, left_operators, right_operators, small, far_small, sector_rows):
     wave_rows, group_rows = sizes[0] * UNIT, sizes[1] * UNIT
     send = functools.partial(lax.ppermute, axis_name=AXES)
     packed = pack_wave(sector_rows, wavefunction, wave_rows)
     got = [send(packed, perm=perm) for perm in GATHER_FIRST]
-    far_small = [send(numbers, perm=OTHER_CORE) for numbers in small]
     far_left = send(left_operators, perm=OTHER_CORE)
     far_right = send(right_operators, perm=OTHER_CORE)
     both, second, first = join(sector_rows, packed, got, group_rows)
@@ -477,8 +459,9 @@
     near = [both, *got]
     far = [send(block, perm=OTHER_CORE) for block in near[:3]]
     far.append(send(near[3], perm=FROM_CORE_0))
-    operators = (left_operators, right_operators, far_left, far_right)
-    own, *sends = term_products(sector_rows, small, far_small, near, far, operators, group_rows)
+    split = (8, 16, 2, TILE, 512)
+    operators = (left_operators.reshape(split), right_operators, far_left.reshape(split), far_right)
+    own, *sends = term_products(sector_rows, small, far_small, near, far, operators, sizes[1])
     got = [send(s, perm=FIRST_AXIS[k + 1]) for k, s in enumerate(sends)]
     return regroup(sector_rows, own, got)
 
@@ -494,7 +477,8 @@
 ):
     small = (source_sector, target_sector, live_terms)
     branches = [functools.partial(sized, sizes) for sizes in SIZES]
-    operands = (wavefunction, left_operators, right_operators, small, sector_rows)
+    far_small = tuple(lax.ppermute(numbers, AXES, OTHER_CORE) for numbers in small)
+    operands = (wavefunction, left_operators, right_operators, small, far_small, sector_rows)
     keep, *sends = lax.switch(choose(sector_rows, SIZES), branches, *operands)
     got = [lax.ppermute(s, AXES, SECOND_AXIS[k + 1]) for k, s in enumerate(sends)]
     parts = spread(keep, got)
@@ -502,8 +486,7 @@
     arrived = lax.all_to_all(
         parts, "term", split_axis=0, concat_axis=0, axis_index_groups=groups, tiled=True
     )
-    keep, give = add_parts(arrived)
-    return finish(sector_rows, keep, lax.ppermute(give, AXES, OTHER_CORE))
+    return finish(sector_rows, arrived)
 
 
 def solution(mesh):

time: 128 us -> 128 us (level)
  blocking collectives: 26.7 us -> 19.9 us
  waiting for transfers between devices: 40.3 us -> 46.1 us
  starting transfers between devices: 37.3 us -> 41.3 us
  Pallas kernels: 18.7 us -> 16 us
    all_to_all x1, blocking collectives: 26.7 us -> 19.9 us  [local(): lax.all_to_all(parts, 'term', split_axis=0, concat_axis=0, axis_index_gro...]
    ppermute x4 -> x3, starting transfers between devices: 6.9 us -> 0.51 us  [local(): lax.ppermute(numbers, AXES, OTHER_CORE)]
    ppermute x3, starting transfers between devices: 6.67 us -> 13 us  [sized(): far = [send(block, perm=OTHER_CORE) for block in near[:3]]]
    ppermute x1, starting transfers between devices: 3.44 us -> 9.65 us  [sized(): far.append(send(near[3], perm=FROM_CORE_0))]
    ppermute x3, waiting for transfers between devices: 4.86 us -> 8.93 us  [sized(): send(block, perm=perm)]
    ppermute x4 -> x3, waiting for transfers between devices: 4.05 us -> 0.01 us  [local(): lax.ppermute(numbers, AXES, OTHER_CORE)]
    ppermute x3, starting transfers between devices: 6.55 us -> 2.9 us  [local(): lax.ppermute(s, AXES, SECOND_AXIS[k + 1])]
    ppermute x3, waiting for transfers between devices: 6.26 us -> 9.12 us  [local(): lax.ppermute(s, AXES, SECOND_AXIS[k + 1])]
  transfers between devices with their start and end apart: 22 -> 21, of which waited for: 12 -> 9; matrix products, arithmetic and copies ran while one was open for 0% -> 0% of each run, Pallas kernels for 2% -> 3%
where the time goes in v1:
time: 128 us; the launch traced here: 126 us
  waiting for transfers between devices  46.1 us (36%)
  starting transfers between devices  41.3 us (32%)
  blocking collectives  19.9 us (16%)
  Pallas kernels  16 us (12%)
    all_to_all x1, blocking collectives, local(): lax.all_to_all(parts, 'term', split_axis=0, concat_axis=0, axis_index_gro...  19.9 us
    ppermute x3, waiting for transfers between devices, sized(): got = [send(s, perm=FIRST_AXIS[k + 1]) for k, s in enumerate(sends)]  17.9 us
    ppermute x3, starting transfers between devices, sized(): far = [send(block, perm=OTHER_CORE) for block in near[:3]]  13 us
    ppermute x1, starting transfers between devices, sized(): far.append(send(near[3], perm=FROM_CORE_0))  9.65 us
    ppermute x3, waiting for transfers between devices, local(): lax.ppermute(s, AXES, SECOND_AXIS[k + 1])  9.12 us
    ppermute x3, waiting for transfers between devices, sized(): send(block, perm=perm)  8.93 us
    ppermute x3, waiting for transfers between devices, sized(): got = [send(packed, perm=perm) for perm in GATHER_FIRST]  7.49 us
    ppermute x3, starting transfers between devices, sized(): send(block, perm=perm)  7.4 us
  transfers between devices with their start and end apart: 21, of which 9 were waited for; matrix products, arithmetic and copies ran while one was open for 0% of the time, Pallas kernels for 3%

profile of v1, /device:TPU:6, one launch (start us, length us, event | category | flops | bytes accessed | tf_op | source)
XLA Modules:
  0.0 125.5 jit_solution(650182924293445282)
XLA Ops:
  0.0 0.0 collective-permute-start.45
  0.0 0.5 collective-permute-start.46
  0.5 0.0 collective-permute-start.47
  0.5 1.3 %choose.1 = s32[1]{0:T(128)} custom-call(s32[16]{0:T(128)} %rows_ref.3), custom_call_target="tpu_custom_call" | custom-call | tf_op jit(solution)/shard_map/choose/pallas_call | solution.py:93
  2.4 0.0 collective-permute-done.47
  2.5 0.0 collective-permute-done.45
  2.5 0.0 collective-permute-done.46
  2.5 86.8 %conditional.1 = ((f32[256,512]{1,0:T(8,128)S(1)}, bf16[256,512]{1,0:T(8,128)(2,1)S(1)}, bf16[256,512]{1,0:T(8,128)(2,1)S(1)}, bf16[256,512]{1,0:T(8,128)(2,1)S(1)})) conditional(s32[]{:T(128)} %bitcast.6, (s32[16]{0:T(128)}, bf16[2,512,512]{2,1,0:T(8,128)(2,1)}, bf16[8,512,512]{2,1,0:T(8,128)(2,1)}, bf16[8,512,512]{2,1,0:T(8,128)(2,1)}, ...), branch_computations={%region_0.0_spmd, %region_1.0_spmd, %region_2.0_spmd} | conditional | flops 8000000000 | bytes 102761648 | solution.py:482
  2.5 0.0 copy-start.5
  2.5 0.0 copy-start.8
  2.5 0.0 copy-start.11
  2.5 0.6 collective-permute-start.25
  3.1 0.3 collective-permute-start.26
  3.4 1.3 %pack_wave.4.own_ref = bf16[896,256]{1,0:T(8,128)(2,1)S(1)} custom-call(s32[16]{0:T(128)} %get-tuple-element.82.rows_ref, bf16[2,512,512]{2,1,0:T(8,128)(2,1)} %get-tuple-element.89.wave_ref), custom_call_target="tpu_custom_call" | custom-call | tf_op jit(solution)/shard_map/cond/branch_1_fun/pack_wave/pallas_call | solution.py:122
  4.8 0.7 collective-permute-start.17
  5.5 0.7 collective-permute-start.16
  6.1 2.3 %collective-permute-start.15 = (bf16[896,256]{1,0:T(8,128)(2,1)S(1)}, bf16[896,256]{1,0:T(8,128)(2,1)S(1)}, u32[]{:S(2)}, u32[]{:S(2)}) collective-permute-start(bf16[896,256]{1,0:T(8,128)(2,1)S(1)} %pack_wave.4.own_ref), channel_id=1, source_target_pairs={{0,17},{8,10},{32,49},{40,42},{64,81},{72,74},{96,113},{104,106},{... | collective-permute-start | bytes 1376264 | tf_op jit(solution)/shard_map/cond/branch_1_fun/ppermute | solution.py:454
  8.4 0.0 collective-permute-done.17.got3
  8.4 0.0 collective-permute-done.16.got2
  8.4 7.5 %collective-permute-done.15.got1 = bf16[896,256]{1,0:T(8,128)(2,1)S(1)} collective-permute-done((bf16[896,256]{1,0:T(8,128)(2,1)S(1)}, bf16[896,256]{1,0:T(8,128)(2,1)S(1)}, u32[]{:S(2)}, u32[]{:S(2)}) %collective-permute-start.15) | collective-permute-done | bytes 458784 | tf_op jit(solution)/shard_map/cond/branch_1_fun/ppermute | solution.py:454
  15.9 1.1 join.4
  17.0 3.4 %collective-permute-start.19 = (bf16[1408,256]{1,0:T(8,128)(2,1)S(1)}, bf16[1408,256]{1,0:T(8,128)(2,1)S(1)}, u32[]{:S(2)}, u32[]{:S(2)}) collective-permute-start(bf16[1408,256]{1,0:T(8,128)(2,1)S(1)} %get-tuple-element.92), channel_id=1, source_target_pairs={{0,4},{8,25},{32,36},{40,57},{64,68},{72,89},{96,100},{104,121},{1... | collective-permute-start | bytes 2162696 | tf_op jit(solution)/shard_map/cond/branch_1_fun/ppermute | solution.py:458
  20.4 2.8 %collective-permute-start.20 = (bf16[1408,256]{1,0:T(8,128)(2,1)S(1)}, bf16[1408,256]{1,0:T(8,128)(2,1)S(1)}, u32[]{:S(2)}, u32[]{:S(2)}) collective-permute-start(bf16[1408,256]{1,0:T(8,128)(2,1)S(1)} %get-tuple-element.91), channel_id=1, source_target_pairs={{0,6},{32,38},{64,70},{96,102},{128,134},{160,166},{192,198},{224,... | collective-permute-start | bytes 2162696 | tf_op jit(solution)/shard_map/cond/branch_1_fun/ppermute | solution.py:458
  23.3 1.2 collective-permute-start.18
  24.4 8.9 %collective-permute-done.19.near2 = bf16[1408,256]{1,0:T(8,128)(2,1)S(1)} collective-permute-done((bf16[1408,256]{1,0:T(8,128)(2,1)S(1)}, bf16[1408,256]{1,0:T(8,128)(2,1)S(1)}, u32[]{:S(2)}, u32[]{:S(2)}) %collective-permute-start.19) | collective-permute-done | bytes 720928 | tf_op jit(solution)/shard_map/cond/branch_1_fun/ppermute | solution.py:458
  33.3 12.9 %collective-permute-start.23 = (bf16[1408,256]{1,0:T(8,128)(2,1)S(1)}, bf16[1408,256]{1,0:T(8,128)(2,1)S(1)}, u32[]{:S(2)}, u32[]{:S(2)}) collective-permute-start(bf16[1408,256]{1,0:T(8,128)(2,1)S(1)} %collective-permute-done.19.near2), channel_id=1, source_target_pairs={{0,8},{8,0},{32,40},{40,32},{64,72},{72,64},{96,104},{104,96},{128... | collective-permute-start | bytes 2162696 | tf_op jit(solution)/shard_map/cond/branch_1_fun/ppermute | solution.py:460
  46.3 0.0 collective-permute-done.20.near3
  46.3 0.0 collective-permute-start.21
  46.3 0.0 collective-permute-done.18.near1
  46.3 9.6 %collective-permute-start.24 = (bf16[1408,256]{1,0:T(8,128)(2,1)S(1)}, bf16[1408,256]{1,0:T(8,128)(2,1)S(1)}, u32[]{:S(2)}, u32[]{:S(2)}) collective-permute-start(bf16[1408,256]{1,0:T(8,128)(2,1)S(1)} %collective-permute-done.20.near3), channel_id=1, source_target_pairs={{0,8},{32,40},{64,72},{96,104},{128,136},{160,168},{192,200},{224,... | collective-permute-start | bytes 2162696 | tf_op jit(solution)/shard_map/cond/branch_1_fun/ppermute | solution.py:461
  56.0 0.0 collective-permute-done.23.far2
  56.0 0.1 collective-permute-start.22
  56.1 1.6 %collective-permute-done.24.far3 = bf16[1408,256]{1,0:T(8,128)(2,1)S(1)} collective-permute-done((bf16[1408,256]{1,0:T(8,128)(2,1)S(1)}, bf16[1408,256]{1,0:T(8,128)(2,1)S(1)}, u32[]{:S(2)}, u32[]{:S(2)}) %collective-permute-start.24) | collective-permute-done | bytes 720928 | tf_op jit(solution)/shard_map/cond/branch_1_fun/ppermute | solution.py:461
  57.7 1.0 collective-permute-done.22.far1
  58.7 0.0 collective-permute-done.21.far0
  58.7 0.0 collective-permute-done.25
  58.7 0.0 collective-permute-done.26.far_right
  58.8 0.0 copy-done.5
  58.8 0.0 copy-done.8
  58.8 0.0 copy-done.11
  58.8 7.3 %term_products.4 = (f32[704,512]{1,0:T(8,128)S(1)}, bf16[704,512]{1,0:T(8,128)(2,1)S(1)}, bf16[704,512]{1,0:T(8,128)(2,1)S(1)}, bf16[704,512]{1,0:T(8,128)(2,1)S(1)}) custom-call(s32[16]{0:T(128)S(1)} %copy-done.5, s32[8]{0:T(128)S(1)} %copy-done.8, s32[8]{0:T(128)S(1)} %copy-done.11, s32[1]{0:T(128)} %get-tuple-element.85.live_ref, ...), custom_call_target="tpu_custom_call" | custom-call | flops 8000000000 | bytes 16777216 | tf_op jit(solution)/shard_map/cond/branch_1_fun/term_products/pallas_call | solution.py:348
  66.1 0.1 collective-permute-start.27
  66.2 2.5 %collective-permute-start.28 = (bf16[704,512]{1,0:T(8,128)(2,1)S(1)}, bf16[704,512]{1,0:T(8,128)(2,1)S(1)}, u32[]{:S(2)}, u32[]{:S(2)}) collective-permute-start(bf16[704,512]{1,0:T(8,128)(2,1)S(1)} %get-tuple-element.97), channel_id=1, source_target_pairs={{0,4},{8,9},{32,36},{40,41},{64,68},{72,73},{96,100},{104,105},{12... | collective-permute-start | bytes 2162696 | tf_op jit(solution)/shard_map/cond/branch_1_fun/ppermute | solution.py:465
  68.7 0.7 collective-permute-start.29
  69.4 17.0 %collective-permute-done.27.got1 = bf16[704,512]{1,0:T(8,128)(2,1)S(1)} collective-permute-done((bf16[704,512]{1,0:T(8,128)(2,1)S(1)}, bf16[704,512]{1,0:T(8,128)(2,1)S(1)}, u32[]{:S(2)}, u32[]{:S(2)}) %collective-permute-start.27) | collective-permute-done | bytes 720928 | tf_op jit(solution)/shard_map/cond/branch_1_fun/ppermute | solution.py:465
  86.4 0.0 collective-permute-done.28.got2
  86.4 0.9 collective-permute-done.29.got3
  87.3 1.5 %regroup.4 = (f32[256,512]{1,0:T(8,128)S(1)}, bf16[256,512]{1,0:T(8,128)(2,1)S(1)}, bf16[256,512]{1,0:T(8,128)(2,1)S(1)}, bf16[256,512]{1,0:T(8,128)(2,1)S(1)}) custom-call(s32[16]{0:T(128)S(1)} %copy-done.5, f32[704,512]{1,0:T(8,128)S(1)} %get-tuple-element.95.own_ref, bf16[704,512]{1,0:T(8,128)(2,1)S(1)} %collective-permute-done.27.got1, ...), custom_call_target="tpu_custom_call" | custom-call | tf_op jit(solution)/shard_map/cond/branch_1_fun/regroup/pallas_call | solution.py:397
  89.3 0.0 copy-start.3
  89.3 1.3 %collective-permute-start.48 = (bf16[256,512]{1,0:T(8,128)(2,1)S(1)}, bf16[256,512]{1,0:T(8,128)(2,1)S(1)}, u32[]{:S(2)}, u32[]{:S(2)}) collective-permute-start(bf16[256,512]{1,0:T(8,128)(2,1)S(1)} %get-tuple-element.121), channel_id=1, source_target_pairs={{0,16},{8,10},{32,48},{40,42},{64,80},{72,74},{96,112},{104,106},{... | collective-permute-start | bytes 786440 | tf_op jit(solution)/shard_map/ppermute | solution.py:483
  90.6 1.6 %collective-permute-start.49 = (bf16[256,512]{1,0:T(8,128)(2,1)S(1)}, bf16[256,512]{1,0:T(8,128)(2,1)S(1)}, u32[]{:S(2)}, u32[]{:S(2)}) collective-permute-start(bf16[256,512]{1,0:T(8,128)(2,1)S(1)} %get-tuple-element.122), channel_id=1, source_target_pairs={{0,1},{8,12},{32,33},{40,44},{64,65},{72,76},{96,97},{104,108},{12... | collective-permute-start | bytes 786440 | tf_op jit(solution)/shard_map/ppermute | solution.py:483
  92.2 0.0 collective-permute-start.50
  92.2 3.6 %collective-permute-done.48.got1 = bf16[256,512]{1,0:T(8,128)(2,1)S(1)} collective-permute-done((bf16[256,512]{1,0:T(8,128)(2,1)S(1)}, bf16[256,512]{1,0:T(8,128)(2,1)S(1)}, u32[]{:S(2)}, u32[]{:S(2)}) %collective-permute-start.48) | collective-permute-done | bytes 262176 | tf_op jit(solution)/shard_map/ppermute | solution.py:483
  95.7 0.0 copy-start
  95.7 2.9 %collective-permute-done.49.got2 = bf16[256,512]{1,0:T(8,128)(2,1)S(1)} collective-permute-done((bf16[256,512]{1,0:T(8,128)(2,1)S(1)}, bf16[256,512]{1,0:T(8,128)(2,1)S(1)}, u32[]{:S(2)}, u32[]{:S(2)}) %collective-permute-start.49) | collective-permute-done | bytes 262176 | tf_op jit(solution)/shard_map/ppermute | solution.py:483
  98.6 0.0 copy-start.1
  98.6 2.7 %collective-permute-done.50.got3 = bf16[256,512]{1,0:T(8,128)(2,1)S(1)} collective-permute-done((bf16[256,512]{1,0:T(8,128)(2,1)S(1)}, bf16[256,512]{1,0:T(8,128)(2,1)S(1)}, u32[]{:S(2)}, u32[]{:S(2)}) %collective-permute-start.50) | collective-permute-done | bytes 262176 | tf_op jit(solution)/shard_map/ppermute | solution.py:483
  101.3 0.0 copy-done
  101.3 0.0 copy-done.1
  101.3 0.7 copy-done.2
  102.0 1.9 %spread.1 = bf16[8,2,16,512]{3,2,1,0:T(8,128)(2,1)} custom-call(f32[256,512]{1,0:T(8,128)S(1)} %get-tuple-element.120.keep_ref, bf16[256,512]{1,0:T(8,128)(2,1)} %copy-done, bf16[256,512]{1,0:T(8,128)(2,1)} %copy-done.1, bf16[256,512]{1,0:T(8,128)(2,1)} %copy-done.2), custom_call_target="tpu_custom_call" | custom-call | tf_op jit(solution)/shard_map/spread/pallas_call | solution.py:420
  104.0 19.9 %all_to_all.5.parts_ref = bf16[8,2,16,512]{3,2,1,0:T(8,128)(2,1)} all-to-all(bf16[8,2,16,512]{3,2,1,0:T(8,128)(2,1)} %spread.1), channel_id=1, replica_groups={{0,32,64,96,128,160,192,224},{8,40,72,104,136,168,200,232},{16,48,80,11..., dimensions={0} | all-to-all | bytes 524288 | tf_op jit(solution)/shard_map/all_to_all | solution.py:486
  123.9 0.0 copy-done.3
  123.9 1.6 %finish.1 = f32[2,16,512]{2,1,0:T(8,128)} custom-call(s32[16]{0:T(128)S(1)} %copy-done.3, bf16[8,2,16,512]{3,2,1,0:T(8,128)(2,1)} %all_to_all.5.parts_ref), custom_call_target="tpu_custom_call" | custom-call | tf_op jit(solution)/shard_map/finish/pallas_call | solution.py:441
  (1 shorter events, 0.0 us)
Async XLA Ops:
  0.0 2.5 %collective-permute-start.45 = (s32[8]{0:T(128)}, s32[8]{0:T(128)S(1)}, u32[]{:S(2)}, u32[]{:S(2)}) collective-permute-start(s32[8]{0:T(128)} %param.13), channel_id=1, source_target_pairs={{0,8},{8,0},{32,40},{40,32},{64,72},{72,64},{96,104},{104,96},{128... | collective-permute-start | bytes 104 | tf_op jit(solution)/shard_map/ppermute | solution.py:480
  0.0 2.5 %collective-permute-start.46 = (s32[8]{0:T(128)}, s32[8]{0:T(128)S(1)}, u32[]{:S(2)}, u32[]{:S(2)}) collective-permute-start(s32[8]{0:T(128)} %param.14), channel_id=1, source_target_pairs={{0,8},{8,0},{32,40},{40,32},{64,72},{72,64},{96,104},{104,96},{128... | collective-permute-start | bytes 104 | tf_op jit(solution)/shard_map/ppermute | solution.py:480
  0.5 1.9 %collective-permute-start.47 = (s32[1]{0:T(128)}, s32[1]{0:T(128)}, u32[]{:S(2)}, u32[]{:S(2)}) collective-permute-start(s32[1]{0:T(128)} %param.15), channel_id=1, source_target_pairs={{0,8},{8,0},{32,40},{40,32},{64,72},{72,64},{96,104},{104,96},{128... | collective-permute-start | bytes 20 | tf_op jit(solution)/shard_map/ppermute | solution.py:480
  2.5 56.3 %copy-start.5 = (s32[16]{0:T(128)S(1)}, s32[16]{0:T(128)}, u32[]{:S(2)}) copy-start(s32[16]{0:T(128)} %get-tuple-element.82.rows_ref) | copy-start | bytes 196 | tf_op jit(solution)/shard_map/cond
  2.5 56.3 %copy-start.8 = (s32[8]{0:T(128)S(1)}, s32[8]{0:T(128)}, u32[]{:S(2)}) copy-start(s32[8]{0:T(128)} %get-tuple-element.83.source_ref) | copy-start | bytes 100 | tf_op jit(solution)/shard_map/cond
  2.5 56.3 %copy-start.11 = (s32[8]{0:T(128)S(1)}, s32[8]{0:T(128)}, u32[]{:S(2)}) copy-start(s32[8]{0:T(128)} %get-tuple-element.84.target_ref) | copy-start | bytes 100 | tf_op jit(solution)/shard_map/cond
  2.5 56.2 %collective-permute-start.25 = (bf16[8,512,512]{2,1,0:T(8,128)(2,1)}, bf16[8,512,512]{2,1,0:T(8,128)(2,1)S(1)}, u32[]{:S(2)}, u32[]{:S(2)}) collective-permute-start(bf16[8,512,512]{2,1,0:T(8,128)(2,1)} %get-tuple-element.93), channel_id=1, source_target_pairs={{0,8},{8,0},{32,40},{40,32},{64,72},{72,64},{96,104},{104,96},{128... | collective-permute-start | bytes 12582920 | tf_op jit(solution)/shard_map/cond/branch_1_fun/ppermute | solution.py:455
  3.1 55.6 %collective-permute-start.26 = (bf16[8,512,512]{2,1,0:T(8,128)(2,1)}, bf16[8,512,512]{2,1,0:T(8,128)(2,1)S(1)}, u32[]{:S(2)}, u32[]{:S(2)}) collective-permute-start(bf16[8,512,512]{2,1,0:T(8,128)(2,1)} %get-tuple-element.94.near_right), channel_id=1, source_target_pairs={{0,8},{8,0},{32,40},{40,32},{64,72},{72,64},{96,104},{104,96},{128... | collective-permute-start | bytes 12582920 | tf_op jit(solution)/shard_map/cond/branch_1_fun/ppermute | solution.py:456
  4.8 3.7 %collective-permute-start.17 = (bf16[896,256]{1,0:T(8,128)(2,1)S(1)}, bf16[896,256]{1,0:T(8,128)(2,1)S(1)}, u32[]{:S(2)}, u32[]{:S(2)}) collective-permute-start(bf16[896,256]{1,0:T(8,128)(2,1)S(1)} %pack_wave.4.own_ref), channel_id=1, source_target_pairs={{8,14},{40,46},{72,78},{104,110},{136,142},{168,174},{200,206},{23... | collective-permute-start | bytes 1376264 | tf_op jit(solution)/shard_map/cond/branch_1_fun/ppermute | solution.py:454
  5.5 3.0 %collective-permute-start.16 = (bf16[896,256]{1,0:T(8,128)(2,1)S(1)}, bf16[896,256]{1,0:T(8,128)(2,1)S(1)}, u32[]{:S(2)}, u32[]{:S(2)}) collective-permute-start(bf16[896,256]{1,0:T(8,128)(2,1)S(1)} %pack_wave.4.own_ref), channel_id=1, source_target_pairs={{8,12},{40,44},{72,76},{104,108},{136,140},{168,172},{200,204},{23... | collective-permute-start | bytes 1376264 | tf_op jit(solution)/shard_map/cond/branch_1_fun/ppermute | solution.py:454
  6.1 9.8 %collective-permute-start.15 = (bf16[896,256]{1,0:T(8,128)(2,1)S(1)}, bf16[896,256]{1,0:T(8,128)(2,1)S(1)}, u32[]{:S(2)}, u32[]{:S(2)}) collective-permute-start(bf16[896,256]{1,0:T(8,128)(2,1)S(1)} %pack_wave.4.own_ref), channel_id=1, source_target_pairs={{0,17},{8,10},{32,49},{40,42},{64,81},{72,74},{96,113},{104,106},{... | collective-permute-start | bytes 1376264 | tf_op jit(solution)/shard_map/cond/branch_1_fun/ppermute | solution.py:454
  17.0 16.3 %collective-permute-start.19 = (bf16[1408,256]{1,0:T(8,128)(2,1)S(1)}, bf16[1408,256]{1,0:T(8,128)(2,1)S(1)}, u32[]{:S(2)}, u32[]{:S(2)}) collective-permute-start(bf16[1408,256]{1,0:T(8,128)(2,1)S(1)} %get-tuple-element.92), channel_id=1, source_target_pairs={{0,4},{8,25},{32,36},{40,57},{64,68},{72,89},{96,100},{104,121},{1... | collective-permute-start | bytes 2162696 | tf_op jit(solution)/shard_map/cond/branch_1_fun/ppermute | solution.py:458
  20.4 25.9 %collective-permute-start.20 = (bf16[1408,256]{1,0:T(8,128)(2,1)S(1)}, bf16[1408,256]{1,0:T(8,128)(2,1)S(1)}, u32[]{:S(2)}, u32[]{:S(2)}) collective-permute-start(bf16[1408,256]{1,0:T(8,128)(2,1)S(1)} %get-tuple-element.91), channel_id=1, source_target_pairs={{0,6},{32,38},{64,70},{96,102},{128,134},{160,166},{192,198},{224,... | collective-permute-start | bytes 2162696 | tf_op jit(solution)/shard_map/cond/branch_1_fun/ppermute | solution.py:458
  23.3 23.0 %collective-permute-start.18 = (bf16[1408,256]{1,0:T(8,128)(2,1)S(1)}, bf16[1408,256]{1,0:T(8,128)(2,1)S(1)}, u32[]{:S(2)}, u32[]{:S(2)}) collective-permute-start(bf16[1408,256]{1,0:T(8,128)(2,1)S(1)} %get-tuple-element.91), channel_id=1, source_target_pairs={{0,2},{8,25},{32,34},{40,57},{64,66},{72,89},{96,98},{104,121},{12... | collective-permute-start | bytes 2162696 | tf_op jit(solution)/shard_map/cond/branch_1_fun/ppermute | solution.py:458
  33.3 22.6 %collective-permute-start.23 = (bf16[1408,256]{1,0:T(8,128)(2,1)S(1)}, bf16[1408,256]{1,0:T(8,128)(2,1)S(1)}, u32[]{:S(2)}, u32[]{:S(2)}) collective-permute-start(bf16[1408,256]{1,0:T(8,128)(2,1)S(1)} %collective-permute-done.19.near2), channel_id=1, source_target_pairs={{0,8},{8,0},{32,40},{40,32},{64,72},{72,64},{96,104},{104,96},{128... | collective-permute-start | bytes 2162696 | tf_op jit(solution)/shard_map/cond/branch_1_fun/ppermute | solution.py:460
  46.3 12.5 %collective-permute-start.21 = (bf16[2816,256]{1,0:T(8,128)(2,1)S(1)}, bf16[2816,256]{1,0:T(8,128)(2,1)S(1)}, u32[]{:S(2)}, u32[]{:S(2)}) collective-permute-start(bf16[2816,256]{1,0:T(8,128)(2,1)S(1)} %get-tuple-element.90.near0), channel_id=1, source_target_pairs={{0,8},{8,0},{32,40},{40,32},{64,72},{72,64},{96,104},{104,96},{128... | collective-permute-start | bytes 4325384 | tf_op jit(solution)/shard_map/cond/branch_1_fun/ppermute | solution.py:460
  46.3 11.4 %collective-permute-start.24 = (bf16[1408,256]{1,0:T(8,128)(2,1)S(1)}, bf16[1408,256]{1,0:T(8,128)(2,1)S(1)}, u32[]{:S(2)}, u32[]{:S(2)}) collective-permute-start(bf16[1408,256]{1,0:T(8,128)(2,1)S(1)} %collective-permute-done.20.near3), channel_id=1, source_target_pairs={{0,8},{32,40},{64,72},{96,104},{128,136},{160,168},{192,200},{224,... | collective-permute-start | bytes 2162696 | tf_op jit(solution)/shard_map/cond/branch_1_fun/ppermute | solution.py:461
  56.0 2.8 %collective-permute-start.22 = (bf16[1408,256]{1,0:T(8,128)(2,1)S(1)}, bf16[1408,256]{1,0:T(8,128)(2,1)S(1)}, u32[]{:S(2)}, u32[]{:S(2)}) collective-permute-start(bf16[1408,256]{1,0:T(8,128)(2,1)S(1)} %collective-permute-done.18.near1), channel_id=1, source_target_pairs={{0,8},{8,0},{32,40},{40,32},{64,72},{72,64},{96,104},{104,96},{128... | collective-permute-start | bytes 2162696 | tf_op jit(solution)/shard_map/cond/branch_1_fun/ppermute | solution.py:460
  66.1 20.3 %collective-permute-start.27 = (bf16[704,512]{1,0:T(8,128)(2,1)S(1)}, bf16[704,512]{1,0:T(8,128)(2,1)S(1)}, u32[]{:S(2)}, u32[]{:S(2)}) collective-permute-start(bf16[704,512]{1,0:T(8,128)(2,1)S(1)} %get-tuple-element.96), channel_id=1, source_target_pairs={{0,2},{8,24},{32,34},{40,56},{64,66},{72,88},{96,98},{104,120},{12... | collective-permute-start | bytes 2162696 | tf_op jit(solution)/shard_map/cond/branch_1_fun/ppermute | solution.py:465
  66.2 20.2 %collective-permute-start.28 = (bf16[704,512]{1,0:T(8,128)(2,1)S(1)}, bf16[704,512]{1,0:T(8,128)(2,1)S(1)}, u32[]{:S(2)}, u32[]{:S(2)}) collective-permute-start(bf16[704,512]{1,0:T(8,128)(2,1)S(1)} %get-tuple-element.97), channel_id=1, source_target_pairs={{0,4},{8,9},{32,36},{40,41},{64,68},{72,73},{96,100},{104,105},{12... | collective-permute-start | bytes 2162696 | tf_op jit(solution)/shard_map/cond/branch_1_fun/ppermute | solution.py:465
  68.7 18.6 %collective-permute-start.29 = (bf16[704,512]{1,0:T(8,128)(2,1)S(1)}, bf16[704,512]{1,0:T(8,128)(2,1)S(1)}, u32[]{:S(2)}, u32[]{:S(2)}) collective-permute-start(bf16[704,512]{1,0:T(8,128)(2,1)S(1)} %get-tuple-element.98), channel_id=1, source_target_pairs={{0,6},{8,25},{32,38},{40,57},{64,70},{72,89},{96,102},{104,121},{1... | collective-permute-start | bytes 2162696 | tf_op jit(solution)/shard_map/cond/branch_1_fun/ppermute | solution.py:465
  89.3 34.6 %copy-start.3 = (s32[16]{0:T(128)S(1)}, s32[16]{0:T(128)}, u32[]{:S(2)}) copy-start(s32[16]{0:T(128)} %rows_ref.3) | copy-start | bytes 196
  89.3 6.4 %collective-permute-start.48 = (bf16[256,512]{1,0:T(8,128)(2,1)S(1)}, bf16[256,512]{1,0:T(8,128)(2,1)S(1)}, u32[]{:S(2)}, u32[]{:S(2)}) collective-permute-start(bf16[256,512]{1,0:T(8,128)(2,1)S(1)} %get-tuple-element.121), channel_id=1, source_target_pairs={{0,16},{8,10},{32,48},{40,42},{64,80},{72,74},{96,112},{104,106},{... | collective-permute-start | bytes 786440 | tf_op jit(solution)/shard_map/ppermute | solution.py:483
  90.6 8.0 %collective-permute-start.49 = (bf16[256,512]{1,0:T(8,128)(2,1)S(1)}, bf16[256,512]{1,0:T(8,128)(2,1)S(1)}, u32[]{:S(2)}, u32[]{:S(2)}) collective-permute-start(bf16[256,512]{1,0:T(8,128)(2,1)S(1)} %get-tuple-element.122), channel_id=1, source_target_pairs={{0,1},{8,12},{32,33},{40,44},{64,65},{72,76},{96,97},{104,108},{12... | collective-permute-start | bytes 786440 | tf_op jit(solution)/shard_map/ppermute | solution.py:483
  92.2 9.1 %collective-permute-start.50 = (bf16[256,512]{1,0:T(8,128)(2,1)S(1)}, bf16[256,512]{1,0:T(8,128)(2,1)S(1)}, u32[]{:S(2)}, u32[]{:S(2)}) collective-permute-start(bf16[256,512]{1,0:T(8,128)(2,1)S(1)} %get-tuple-element.123), channel_id=1, source_target_pairs={{0,17},{8,14},{32,49},{40,46},{64,81},{72,78},{96,113},{104,110},{... | collective-permute-start | bytes 786440 | tf_op jit(solution)/shard_map/ppermute | solution.py:483
  95.7 5.6 %copy-start = (bf16[256,512]{1,0:T(8,128)(2,1)}, bf16[256,512]{1,0:T(8,128)(2,1)S(1)}, u32[]{:S(2)}) copy-start(bf16[256,512]{1,0:T(8,128)(2,1)S(1)} %collective-permute-done.48.got1) | copy-start | bytes 786436
  98.6 2.7 %copy-start.1 = (bf16[256,512]{1,0:T(8,128)(2,1)}, bf16[256,512]{1,0:T(8,128)(2,1)S(1)}, u32[]{:S(2)}) copy-start(bf16[256,512]{1,0:T(8,128)(2,1)S(1)} %collective-permute-done.49.got2) | copy-start | bytes 786436
  101.3 0.7 copy-start.2

commit v2 on v1

--- a/solution.py
+++ b/solution.py
@@ -11,7 +11,7 @@
 TILE = 16
 AXES = ("term", "sector")
 DEPTH = 3
-SIZES = ((25, 38), (28, 44), (32, 64))
+SIZES = ((21, 38), (25, 42), (29, 48), (32, 64))
 
 
 def device_index(x, y, z, core):
@@ -21,23 +21,15 @@
 
 def pairs(move):
     every = [(x, y, z, c) for x in range(4) for y in range(4) for z in range(8) for c in range(2)]
-    return [(device_index(*at), device_index(*move(*at))) for at in every if move(*at) is not None]
+    return [(device_index(*at), device_index(*move(*at))) for at in every]
 
 
 OTHER_CORE = pairs(lambda x, y, z, c: (x, y, z, 1 - c))
-FIRST_AXIS = [pairs(lambda x, y, z, c: (x + k * c, y + k * (1 - c), z, c)) for k in range(4)]
-ACROSS = (3, 2, 1, 0)
-GATHER_FIRST = [
-    pairs(lambda x, y, z, c: (x, y + 1, z, c) if c else (ACROSS[x], y, z, c)),
-    pairs(lambda x, y, z, c: (x, y + 2, z, c) if c else None),
-    pairs(lambda x, y, z, c: (x, y + 3, z, c) if c else None),
+FIRST_AXIS = [
+    pairs(lambda x, y, z, c: (x + 2, y, z, 1) if c else (x, y + 2, z, 0)),
+    pairs(lambda x, y, z, c: (3 - x, y, z, 1) if c else (x, y + 1, z, 0)),
+    pairs(lambda x, y, z, c: (x ^ 1, y, z, 1) if c else (x, y + 3, z, 0)),
 ]
-GATHER_SECOND = [
-    pairs(lambda x, y, z, c: (ACROSS[x], y, z, c) if c else (x, y + 1, z, c)),
-    pairs(lambda x, y, z, c: (ACROSS[x], y, z, c) if c else (x, y + 2, z, c)),
-    pairs(lambda x, y, z, c: None if c else (x, y + 3, z, c)),
-]
-FROM_CORE_0 = pairs(lambda x, y, z, c: None if c else (x, y, z, 1))
 SECOND_AXIS = [pairs(lambda x, y, z, c: (x + k * (1 - c), y + k * c, z, c)) for k in range(4)]
 
 
@@ -76,12 +68,11 @@
     units = [units_of(rows_ref[q]) for q in range(16)]
     pair = functools.reduce(jnp.maximum, [units[q] + units[q + 1] for q in range(0, 16, 2)])
     along_y = functools.reduce(jnp.maximum, [sum(units[q : q + 4]) for q in range(0, 16, 4)])
-    along_x, across = jnp.int32(0), jnp.int32(0)
+    along_x = jnp.int32(0)
     for x_hi in range(2):
         mine = [units[q] for q in range(16) if (q // 2) % 2 == x_hi]
-        across = jnp.maximum(across, sum(mine))
         along_x = jnp.maximum(along_x, sum(lax.div(n + 1, 2) for n in mine))
-    group = jnp.maximum(jnp.maximum(along_y, along_x), lax.div(across + 1, 2))
+    group = jnp.maximum(along_y, along_x)
     chosen = jnp.int32(len(sizes) - 1)
     for i in reversed(range(len(sizes) - 1)):
         chosen = jnp.where((pair <= sizes[i][0]) & (group <= sizes[i][1]), i, chosen)
@@ -129,90 +120,52 @@
     )(sector_rows, wavefunction)
 
 
-def join_kernel(rows_ref, own_ref, got1, got2, got3, both_ref, send2_ref, send1_ref):
-    x, y, _, core = coordinates()
-    x_hi = lax.div(x, 2)
-    block_rows = send1_ref.shape[0]
-
-    def one_pair(p, filled):
-        pair = jnp.where(core == 0, 2 * y + p, 2 * p + x_hi)
-        count = units_of(rows_ref[2 * pair]) + units_of(rows_ref[2 * pair + 1])
-        count = jnp.where((core == 0) & (p >= 2), 0, count)
-        from_x = jnp.where(p == x_hi, 0, 1)
-        k = jnp.where(core == 0, from_x, lax.rem(y - p + 4, 4))
-        for source, block in enumerate((own_ref, got1, got2, got3)):
-
-            @pl.loop(0, jnp.where(k == source, count, 0))
-            def _(u):
-                both_ref[unit_at(filled + u), :] = block[unit_at(u), :]
-
-        return filled + count
-
-    lax.fori_loop(0, 4, one_pair, 0)
-    send1_ref[...] = both_ref[:block_rows]
-
-    @pl.when(core == 0)
-    def _():
-        send2_ref[...] = both_ref[:block_rows]
-
-    @pl.when(core == 1)
-    def _():
-        send2_ref[...] = both_ref[block_rows:]
-
-
-def join(sector_rows, own, got, rows):
-    vmem = pl.BlockSpec(memory_space=pltpu.VMEM)
-    block = jax.ShapeDtypeStruct((rows, 256), jnp.bfloat16)
-    return pl.pallas_call(
-        join_kernel,
-        out_shape=(jax.ShapeDtypeStruct((2 * rows, 256), jnp.bfloat16), block, block),
-        in_specs=[pl.BlockSpec(memory_space=pltpu.SMEM)] + [vmem] * 4,
-        out_specs=(vmem,) * 3,
-        compiler_params=pltpu.CompilerParams(vmem_limit_bytes=24 * 1024 * 1024),
-        name="join",
-    )(sector_rows, own, *got)
-
-
 def terms_kernel(
-    block_units,
+    ahead,
     rows_ref,
-    source_ref,
-    target_ref,
-    live_ref,
-    far_source_ref,
-    far_target_ref,
-    far_live_ref,
-    near0,
-    near1,
-    near2,
-    near3,
-    far0,
-    far1,
-    far2,
-    far3,
+    near_wave,
+    far_wave,
     near_left,
     near_right,
     far_left,
     far_right,
-    own_ref,
-    send1,
-    send2,
-    send3,
+    first_dest,
+    second_dest,
     acc,
     left_buf,
     right_buf,
     wave_buf,
+    chosen,
     sems,
 ):
     x, y, _, core = coordinates()
-    near_live = live_ref[0]
-    total = near_live + far_live_ref[0]
-
-    def facts(i):
+    near_live = rows_ref[32]
+
+    def is_mine(target):
+        to_y = lax.rem(lax.div(target, 4) - y + 4, 4)
+        far_y = (to_y == 1) | (to_y == 2)
+        far_x = lax.rem(lax.div(target, 2), 2) != lax.div(x, 2)
+        return jnp.where(core == 0, far_y, far_x) == ahead
+
+    def note(i, found):
         near = i < near_live
         slot = jnp.where(near, i, i - near_live)
-        source = jnp.where(near, source_ref[slot], far_source_ref[slot])
-        target = jnp.where(near, target_ref[slot], far_target_ref[slot])
+        mine = is_mine(rows_ref[jnp.where(near, 24, 41) + slot])
+
+        @pl.when(mine)
+        def _():
+            chosen[found] = i
+
+        return found + mine.astype(jnp.int32)
+
+    total = lax.fori_loop(0, near_live + rows_ref[49], note, 0)
+
+    def facts(i):
+        i = chosen[i]
+        near = i < near_live
+        slot = jnp.where(near, i, i - near_live)
+        source = rows_ref[jnp.where(near, 16, 33) + slot]
+        target = rows_ref[jnp.where(near, 24, 41) + slot]
         return near, slot, source, target
 
     def copies(near, slot, buf):
@@ -242,41 +195,19 @@
 
     for q in range(16):
 
-        @pl.loop(0, units_of(rows_ref[q]))
+        @pl.loop(0, jnp.where(is_mine(jnp.int32(q)), units_of(rows_ref[q]), 0))
         def _(u):
             acc[tile_at(q * 16 + u), :] = jnp.zeros((TILE, 512), jnp.float32)
 
     def fetch(source, units):
-        source_y = lax.div(source, 4)
         pair = lax.div(source, 2)
-        odd = lax.rem(source, 2)
-        before_odd = jnp.where(odd == 1, units_of(rows_ref[2 * pair]), 0)
-        k = lax.rem(y - source_y + 4, 4)
-        before = jnp.where(
-            lax.rem(pair, 2) == 1, units_of(rows_ref[4 * source_y]) + units_of(rows_ref[4 * source_y + 1]), 0
-        )
-        in_y = jnp.where(k == 0, 0, k + 1) * block_units + before + before_odd
-        source_hi = lax.rem(pair, 2)
-        before = before_odd
-        for p in range(3):
-            both = units_of(rows_ref[4 * p + 2 * source_hi]) + units_of(rows_ref[4 * p + 2 * source_hi + 1])
-            before = before + jnp.where(p < source_y, both, 0)
-        in_x = jnp.where(source_hi == lax.div(x, 2), 0, 2) * block_units + before
-        for memory, layout, half in (
-            ((near0, near1, near2, near3), core, core),
-            ((far0, far1, far2, far3), 1 - core, 1 - core),
-        ):
-            first = jnp.where(layout == 0, in_y, in_x)
-            low = 0
-            for block in memory:
-                high = low + block.shape[0] // UNIT
-                begin_at, end_at = jnp.maximum(first, low), jnp.minimum(first + units, high)
-
-                @pl.loop(begin_at, end_at)
-                def _(u):
-                    wave_buf[half, unit_at(u - first), :] = block[unit_at(u - low), :]
-
-                low = high
+        before = jnp.where(lax.rem(source, 2) == 1, units_of(rows_ref[2 * pair]), 0)
+        first = pair * (near_wave.shape[0] // (8 * UNIT)) + before
+
+        @pl.loop(0, units)
+        def _(u):
+            wave_buf[core, unit_at(u), :] = near_wave[unit_at(first + u), :]
+            wave_buf[1 - core, unit_at(u), :] = far_wave[unit_at(first + u), :]
 
     def clear_tail(source_rows, depth):
         last = units_of(source_rows) - 1
@@ -322,9 +253,11 @@
                 pl.when(target_rows <= 256)(functools.partial(product, 8, depth))
                 pl.when(target_rows > 256)(functools.partial(product, 16, depth))
 
-    place = jnp.where(core == 0, y, x)
-    for k, dest in enumerate((own_ref, send1, send2, send3)):
-        there = lax.rem(place + k, 4)
+    if ahead:
+        places = (lax.rem(jnp.where(core == 0, y, x) + 2, 4), jnp.where(core == 0, lax.rem(y + 1, 4), 3 - x))
+    else:
+        places = (jnp.where(core == 0, lax.rem(y + 3, 4), x + 1 - 2 * lax.rem(x, 2)), jnp.where(core == 0, y, x))
+    for there, dest in zip(places, (first_dest, second_dest)):
 
         def one_sector(i, filled):
             sector, first, step = group_entry(core, there, i)
@@ -340,27 +273,29 @@
         lax.fori_loop(0, 8, one_sector, 0)
 
 
-def term_products(rows, small, far_small, near, far, operators, group_units):
+def term_products(numbers, near, far, operators, group_units, ahead):
     smem = pl.BlockSpec(memory_space=pltpu.SMEM)
     hbm = pl.BlockSpec(memory_space=pltpu.HBM)
     vmem = pl.BlockSpec(memory_space=pltpu.VMEM)
     send = jax.ShapeDtypeStruct((group_units * TILE, 512), jnp.bfloat16)
-    return pl.pallas_call(
-        functools.partial(terms_kernel, group_units),
-        out_shape=(jax.ShapeDtypeStruct((group_units * TILE, 512), jnp.float32), send, send, send),
-        in_specs=[smem] * 7 + [vmem] * 8 + [hbm] * 4,
-        out_specs=(vmem,) * 4,
+    last = send if ahead else jax.ShapeDtypeStruct((group_units * TILE, 512), jnp.float32)
+    return pl.pallas_call(
+        functools.partial(terms_kernel, ahead),
+        out_shape=(send, last),
+        in_specs=[smem] + [vmem] * 2 + [hbm] * 4,
+        out_specs=(vmem,) * 2,
         scratch_shapes=[
             pltpu.VMEM((16 * 256, 512), jnp.float32),
             pltpu.VMEM((DEPTH, 16, TILE, 512), jnp.bfloat16),
             pltpu.VMEM((DEPTH, 512, 512), jnp.bfloat16),
             pltpu.VMEM((2, 512, 256), jnp.bfloat16),
+            pltpu.SMEM((16,), jnp.int32),
             pltpu.SemaphoreType.DMA((DEPTH, 2)),
         ],
-        compiler_params=pltpu.CompilerParams(vmem_limit_bytes=30 * 1024 * 1024),
-        cost_estimate=pl.CostEstimate(flops=8 * 10**9, bytes_accessed=16 * 2**20, transcendentals=0),
-        name="term_products",
-    )(rows, *small, *far_small, *near, *far, *operators)
+        compiler_params=pltpu.CompilerParams(vmem_limit_bytes=46 * 1024 * 1024),
+        cost_estimate=pl.CostEstimate(flops=4 * 10**9, bytes_accessed=8 * 2**20, transcendentals=0),
+        name="terms_ahead" if ahead else "terms_here",
+    )(numbers, near, far, *operators)
 
 
 def regroup_kernel(rows_ref, own_ref, got1, got2, got3, keep_ref, send1, send2, send3, blocks):
@@ -448,21 +383,20 @@
 
 
 def sized(sizes, wavefunction, left_operators, right_operators, small, far_small, sector_rows):
-    wave_rows, group_rows = sizes[0] * UNIT, sizes[1] * UNIT
     send = functools.partial(lax.ppermute, axis_name=AXES)
-    packed = pack_wave(sector_rows, wavefunction, wave_rows)
-    got = [send(packed, perm=perm) for perm in GATHER_FIRST]
+    packed = pack_wave(sector_rows, wavefunction, sizes[0] * UNIT)
+    packed = jnp.broadcast_to(packed, (8, *packed.shape))
     far_left = send(left_operators, perm=OTHER_CORE)
     far_right = send(right_operators, perm=OTHER_CORE)
-    both, second, first = join(sector_rows, packed, got, group_rows)
-    got = [send(block, perm=perm) for block, perm in zip((first, second, first), GATHER_SECOND)]
-    near = [both, *got]
-    far = [send(block, perm=OTHER_CORE) for block in near[:3]]
-    far.append(send(near[3], perm=FROM_CORE_0))
+    near = lax.all_to_all(packed, "sector", split_axis=0, concat_axis=0, tiled=True).reshape(-1, 256)
+    far = send(near, perm=OTHER_CORE)
     split = (8, 16, 2, TILE, 512)
     operators = (left_operators.reshape(split), right_operators, far_left.reshape(split), far_right)
-    own, *sends = term_products(sector_rows, small, far_small, near, far, operators, sizes[1])
-    got = [send(s, perm=FIRST_AXIS[k + 1]) for k, s in enumerate(sends)]
+    numbers = jnp.concatenate([sector_rows, *small, *far_small])
+    terms = functools.partial(term_products, numbers, near, far, operators, sizes[1])
+    got = [send(block, perm=perm) for block, perm in zip(terms(True), FIRST_AXIS)]
+    last, own = terms(False)
+    got.append(send(last, perm=FIRST_AXIS[2]))
     return regroup(sector_rows, own, got)
 
 

time: 128 us -> 135 us (1.055); the launches traced: 126 us -> 134 us
  starting transfers between devices: 41.3 us -> 16.9 us
  waiting for transfers between devices: 46.1 us -> 67.7 us
  Pallas kernels: 16 us -> 25.6 us
  local copies, waits for them, and re-layouts: 0.74 us -> 4.13 us
    all_to_all x0 -> x1, waiting for transfers between devices: none -> 44.3 us  [sized(): lax.all_to_all(packed, 'sector', split_axis=0, concat_axis=0, tiled=True)]
    ppermute x10 -> x2, starting transfers between devices: 29.6 us -> 1.01 us  [the longest x1 1.01 us: sized(): got.append(send(last, perm=FIRST_AXIS[2]))]
    ppermute x10 -> x2, waiting for transfers between devices: 28.1 us -> 7 us  [the longest x1 5.55 us: sized(): far = send(near, perm=OTHER_CORE)]
    pallas_call x2, Pallas kernels: 8.42 us -> 17 us  [term_products(): pl.pallas_call(functools.partial(terms_kernel, ahead), out_shape=(send, l...]
    all_to_all x0 -> x1, starting transfers between devices: none -> 7.5 us  [sized(): lax.all_to_all(packed, 'sector', split_axis=0, concat_axis=0, tiled=True)]
    ppermute x3 -> x2, starting transfers between devices: 7.4 us -> 2.15 us  [sized(): send(block, perm=perm)]
    ppermute x3, starting transfers between devices: 2.9 us -> 5.26 us  [local(): lax.ppermute(s, AXES, SECOND_AXIS[k + 1])]
    ppermute x3, waiting for transfers between devices: 9.12 us -> 6.81 us  [local(): lax.ppermute(s, AXES, SECOND_AXIS[k + 1])]
  transfers between devices with their start and end apart: 21 -> 13, of which waited for: 9 -> 8; matrix products, arithmetic and copies ran while one was open for 0% -> 1% of each run, Pallas kernels for 3% -> 8%
where the time goes in v2:
time: 135 us; the launch traced here: 134 us
  waiting for transfers between devices  67.7 us (50%)
  Pallas kernels  25.6 us (19%)
  blocking collectives  18.8 us (14%)
  starting transfers between devices  16.9 us (13%)
  local copies, waits for them, and re-layouts  4.13 us (3%)
    all_to_all x1, waiting for transfers between devices, sized(): lax.all_to_all(packed, 'sector', split_axis=0, concat_axis=0, tiled=True)  44.3 us
    all_to_all x1, blocking collectives, local(): lax.all_to_all(parts, 'term', split_axis=0, concat_axis=0, axis_index_gro...  18.8 us
    pallas_call x2, Pallas kernels, term_products(): pl.pallas_call(functools.partial(terms_kernel, ahead), out_shape=(send, l...  17 us
    ppermute x2, waiting for transfers between devices, sized(): send(block, perm=perm)  9.61 us
    all_to_all x1, starting transfers between devices, sized(): lax.all_to_all(packed, 'sector', split_axis=0, concat_axis=0, tiled=True)  7.5 us
    ppermute x3, waiting for transfers between devices, local(): lax.ppermute(s, AXES, SECOND_AXIS[k + 1])  6.81 us
    ppermute x1, waiting for transfers between devices, sized(): far = send(near, perm=OTHER_CORE)  5.55 us
    ppermute x3, starting transfers between devices, local(): lax.ppermute(s, AXES, SECOND_AXIS[k + 1])  5.26 us
  transfers between devices with their start and end apart: 13, of which 8 were waited for; matrix products, arithmetic and copies ran while one was open for 1% of the time, Pallas kernels for 8%

profile of v2, /device:TPU:6, one launch (start us, length us, event | category | flops | bytes accessed | tf_op | source)
XLA Modules:
  0.0 134.2 jit_solution(13354455908269956417)
XLA Ops:
  0.0 0.0 collective-permute-start.24
  0.0 0.5 collective-permute-start.25
  0.5 0.0 collective-permute-start.26
  0.5 1.3 choose.1
  2.4 0.0 collective-permute-done.26
  2.4 0.0 collective-permute-done.24
  2.5 0.0 collective-permute-done.25
  2.5 96.6 %conditional.1 = ((f32[256,512]{1,0:T(8,128)S(1)}, bf16[256,512]{1,0:T(8,128)(2,1)}, bf16[256,512]{1,0:T(8,128)(2,1)}, bf16[256,512]{1,0:T(8,128)(2,1)})) conditional(s32[]{:T(128)} %bitcast.12, (s32[16]{0:T(128)}, s32[8]{0:T(128)}, s32[8]{0:T(128)}, s32[1]{0:T(128)}, s32[8]{0:T(128)S(1)}, /*index=5*/s32[8]{0:T(128)S(1)}, ...), branch_computations={%region_0.0_spmd, %region_1.0_spmd, %region_2.0_spmd, %region_3.0_... | conditional | flops 8000000000 | bytes 107431192 | solution.py:416
  2.7 1.4 %pack_wave.6 = bf16[928,256]{1,0:T(8,128)(2,1)S(1)} custom-call(s32[16]{0:T(128)} %get-tuple-element.113.rows_ref, bf16[2,512,512]{2,1,0:T(8,128)(2,1)} %get-tuple-element.120.wave_ref), custom_call_target="tpu_custom_call" | custom-call | tf_op jit(solution)/shard_map/cond/branch_2_fun/pack_wave/pallas_call | solution.py:113
  4.1 2.1 %broadcast_in_dim.10 = bf16[8,928,256]{2,1,0:T(8,128)(2,1)} broadcast(bf16[928,256]{1,0:T(8,128)(2,1)S(1)} %pack_wave.6), dimensions={1,2} | broadcast | bytes 4276224 | tf_op jit(solution)/shard_map/cond/branch_2_fun/broadcast_in_dim | solution.py:388
  6.2 0.0 copy-start.8
  6.2 0.0 copy-start.12
  6.2 0.0 copy-start.16
  6.2 7.5 %all-to-all-start.2 = ((bf16[8,928,256]{2,1,0:T(8,128)(2,1)}), bf16[8,928,256]{2,1,0:T(8,128)(2,1)}, u32[]{:S(2)}, u32[]{:S(2)}) async-start(bf16[8,928,256]{2,1,0:T(8,128)(2,1)} %broadcast_in_dim.10), calls=%async_computation.2 | async-start | bytes 7602176 | tf_op jit(solution)/shard_map/cond/branch_2_fun/all_to_all | solution.py:391
  13.7 0.0 collective-permute-start.14
  13.7 0.5 collective-permute-start.13
  14.2 44.3 %all-to-all-done.2 = bf16[8,928,256]{2,1,0:T(8,128)(2,1)} async-done(((bf16[8,928,256]{2,1,0:T(8,128)(2,1)}), bf16[8,928,256]{2,1,0:T(8,128)(2,1)}, u32[]{:S(2)}, u32[]{:S(2)}) %all-to-all-start.2) | async-done | bytes 3801120 | tf_op jit(solution)/shard_map/cond/branch_2_fun/all_to_all | solution.py:391
  58.5 0.0 collective-permute-start.12
  58.5 0.0 copy-done.8
  58.5 0.0 copy-done.12
  58.5 0.0 copy-done.16
  58.5 1.4 %concatenate.10.rows_ref = s32[50]{0:T(128)S(1)} concatenate(s32[16]{0:T(128)S(1)} %copy-done.8, s32[8]{0:T(128)S(1)} %copy-done.12, s32[8]{0:T(128)S(1)} %copy-done.16, s32[1]{0:T(128)} %get-tuple-element.116, s32[8]{0:T(128)S(1)} %get-tuple-element.117, s32[8]{0:T(128)S(1)} %get-tuple-element.118, s32[1]{0:T(128)} %get-tuple-element.119), dimensions={0} | concatenate | bytes 400 | tf_op jit(solution)/shard_map/cond/branch_2_fun/concatenate | solution.py:395
  59.9 0.0 collective-permute-done.14.far_right
  59.9 0.0 collective-permute-done.13
  59.9 5.6 %collective-permute-done.12.far_wave = bf16[7424,256]{1,0:T(8,128)(2,1)} collective-permute-done((bf16[7424,256]{1,0:T(8,128)(2,1)}, bf16[7424,256]{1,0:T(8,128)(2,1)}, u32[]{:S(2)}, u32[]{:S(2)}) %collective-permute-start.12) | collective-permute-done | bytes 3801120 | tf_op jit(solution)/shard_map/cond/branch_2_fun/ppermute | solution.py:392
  65.4 0.0 copy-start.2
  65.4 7.8 %terms_ahead.6 = (bf16[768,512]{1,0:T(8,128)(2,1)S(1)}, bf16[768,512]{1,0:T(8,128)(2,1)S(1)}) custom-call(s32[50]{0:T(128)S(1)} %concatenate.10.rows_ref, bf16[7424,256]{1,0:T(8,128)(2,1)} %bitcast.6.near_wave, bf16[7424,256]{1,0:T(8,128)(2,1)} %collective-permute-done.12.far_wave, bf16[8,16,2,16,512]{4,3,2,1,0:T(8,128)(2,1)} %bitcast.23, ...), custom_call_target="tpu_custom_call" | custom-call | flops 4000000000 | bytes 8388608 | tf_op jit(solution)/shard_map/cond/branch_2_fun/terms_ahead/pallas_call | solution.py:282
  73.2 2.1 %collective-permute-start.15 = (bf16[768,512]{1,0:T(8,128)(2,1)S(1)}, bf16[768,512]{1,0:T(8,128)(2,1)S(1)}, u32[]{:S(2)}, u32[]{:S(2)}) collective-permute-start(bf16[768,512]{1,0:T(8,128)(2,1)S(1)} %get-tuple-element.124), channel_id=1, source_target_pairs={{0,4},{8,9},{32,36},{40,41},{64,68},{72,73},{96,100},{104,105},{12... | collective-permute-start | bytes 2359304 | tf_op jit(solution)/shard_map/cond/branch_2_fun/ppermute | solution.py:397
  75.4 0.0 collective-permute-start.16
  75.4 0.0 copy-done.2
  75.4 9.2 %terms_here.6 = (bf16[768,512]{1,0:T(8,128)(2,1)S(1)}, f32[768,512]{1,0:T(8,128)S(1)}) custom-call(s32[50]{0:T(128)S(1)} %concatenate.10.rows_ref, bf16[7424,256]{1,0:T(8,128)(2,1)} %bitcast.6.near_wave, bf16[7424,256]{1,0:T(8,128)(2,1)} %collective-permute-done.12.far_wave, bf16[8,16,2,16,512]{4,3,2,1,0:T(8,128)(2,1)S(1)} %bitcast.24, ...), custom_call_target="tpu_custom_call" | custom-call | flops 4000000000 | bytes 8388608 | tf_op jit(solution)/shard_map/cond/branch_2_fun/terms_here/pallas_call | solution.py:282
  84.6 1.0 collective-permute-start.17
  85.6 1.3 collective-permute-done.15.got1
  86.9 8.3 %collective-permute-done.16.got2 = bf16[768,512]{1,0:T(8,128)(2,1)S(1)} collective-permute-done((bf16[768,512]{1,0:T(8,128)(2,1)S(1)}, bf16[768,512]{1,0:T(8,128)(2,1)S(1)}, u32[]{:S(2)}, u32[]{:S(2)}) %collective-permute-start.16) | collective-permute-done | bytes 786464 | tf_op jit(solution)/shard_map/cond/branch_2_fun/ppermute | solution.py:397
  95.2 1.5 %collective-permute-done.17.got3 = bf16[768,512]{1,0:T(8,128)(2,1)S(1)} collective-permute-done((bf16[768,512]{1,0:T(8,128)(2,1)S(1)}, bf16[768,512]{1,0:T(8,128)(2,1)S(1)}, u32[]{:S(2)}, u32[]{:S(2)}) %collective-permute-start.17) | collective-permute-done | bytes 786464 | tf_op jit(solution)/shard_map/cond/branch_2_fun/ppermute | solution.py:399
  96.7 2.4 %regroup.6 = (f32[256,512]{1,0:T(8,128)S(1)}, bf16[256,512]{1,0:T(8,128)(2,1)}, bf16[256,512]{1,0:T(8,128)(2,1)}, bf16[256,512]{1,0:T(8,128)(2,1)}) custom-call(s32[16]{0:T(128)S(1)} %copy-done.8, f32[768,512]{1,0:T(8,128)S(1)} %get-tuple-element.123.own_ref, bf16[768,512]{1,0:T(8,128)(2,1)S(1)} %collective-permute-done.15.got1, ...), custom_call_target="tpu_custom_call" | custom-call | tf_op jit(solution)/shard_map/cond/branch_2_fun/regroup/pallas_call | solution.py:332
  99.1 1.2 collective-permute-start.27
  100.3 2.7 %collective-permute-start.28 = (bf16[256,512]{1,0:T(8,128)(2,1)}, bf16[256,512]{1,0:T(8,128)(2,1)S(1)}, u32[]{:S(2)}, u32[]{:S(2)}) collective-permute-start(bf16[256,512]{1,0:T(8,128)(2,1)} %get-tuple-element.147), channel_id=1, source_target_pairs={{0,1},{8,12},{32,33},{40,44},{64,65},{72,76},{96,97},{104,108},{12... | collective-permute-start | bytes 786440 | tf_op jit(solution)/shard_map/ppermute | solution.py:417
  102.9 1.4 %collective-permute-start.29 = (bf16[256,512]{1,0:T(8,128)(2,1)}, bf16[256,512]{1,0:T(8,128)(2,1)S(1)}, u32[]{:S(2)}, u32[]{:S(2)}) collective-permute-start(bf16[256,512]{1,0:T(8,128)(2,1)} %get-tuple-element.148), channel_id=1, source_target_pairs={{0,17},{8,14},{32,49},{40,46},{64,81},{72,78},{96,113},{104,110},{... | collective-permute-start | bytes 786440 | tf_op jit(solution)/shard_map/ppermute | solution.py:417
  104.4 1.3 collective-permute-done.27.got1
  105.7 0.0 copy-start.3
  105.7 2.7 %collective-permute-done.28.got2 = bf16[256,512]{1,0:T(8,128)(2,1)S(1)} collective-permute-done((bf16[256,512]{1,0:T(8,128)(2,1)}, bf16[256,512]{1,0:T(8,128)(2,1)S(1)}, u32[]{:S(2)}, u32[]{:S(2)}) %collective-permute-start.28) | collective-permute-done | bytes 262176 | tf_op jit(solution)/shard_map/ppermute | solution.py:417
  108.4 0.0 copy-start.4
  108.4 2.8 %collective-permute-done.29.got3 = bf16[256,512]{1,0:T(8,128)(2,1)S(1)} collective-permute-done((bf16[256,512]{1,0:T(8,128)(2,1)}, bf16[256,512]{1,0:T(8,128)(2,1)S(1)}, u32[]{:S(2)}, u32[]{:S(2)}) %collective-permute-start.29) | collective-permute-done | bytes 262176 | tf_op jit(solution)/shard_map/ppermute | solution.py:417
  111.2 0.0 copy-start.5
  111.2 0.0 copy-done.3
  111.2 0.0 copy-done.4
  111.2 0.7 copy-done.5
  111.9 1.9 %spread.1 = bf16[8,2,16,512]{3,2,1,0:T(8,128)(2,1)} custom-call(f32[256,512]{1,0:T(8,128)S(1)} %get-tuple-element.145.keep_ref, bf16[256,512]{1,0:T(8,128)(2,1)} %copy-done.3, bf16[256,512]{1,0:T(8,128)(2,1)} %copy-done.4, bf16[256,512]{1,0:T(8,128)(2,1)} %copy-done.5), custom_call_target="tpu_custom_call" | custom-call | tf_op jit(solution)/shard_map/spread/pallas_call | solution.py:355
  113.8 18.8 %all_to_all.21.parts_ref = bf16[8,2,16,512]{3,2,1,0:T(8,128)(2,1)} all-to-all(bf16[8,2,16,512]{3,2,1,0:T(8,128)(2,1)} %spread.1), channel_id=1, replica_groups={{0,32,64,96,128,160,192,224},{8,40,72,104,136,168,200,232},{16,48,80,11..., dimensions={0} | all-to-all | bytes 524288 | tf_op jit(solution)/shard_map/all_to_all | solution.py:420
  132.6 1.6 %finish.1 = f32[2,16,512]{2,1,0:T(8,128)} custom-call(s32[16]{0:T(128)} %rows_ref.3, bf16[8,2,16,512]{3,2,1,0:T(8,128)(2,1)} %all_to_all.21.parts_ref), custom_call_target="tpu_custom_call" | custom-call | tf_op jit(solution)/shard_map/finish/pallas_call | solution.py:376
Async XLA Ops:
  0.0 2.5 %collective-permute-start.24 = (s32[8]{0:T(128)}, s32[8]{0:T(128)S(1)}, u32[]{:S(2)}, u32[]{:S(2)}) collective-permute-start(s32[8]{0:T(128)} %param.14), channel_id=1, source_target_pairs={{0,8},{8,0},{32,40},{40,32},{64,72},{72,64},{96,104},{104,96},{128... | collective-permute-start | bytes 104 | tf_op jit(solution)/shard_map/ppermute | solution.py:414
  0.0 2.5 %collective-permute-start.25 = (s32[8]{0:T(128)}, s32[8]{0:T(128)S(1)}, u32[]{:S(2)}, u32[]{:S(2)}) collective-permute-start(s32[8]{0:T(128)} %param.15), channel_id=1, source_target_pairs={{0,8},{8,0},{32,40},{40,32},{64,72},{72,64},{96,104},{104,96},{128... | collective-permute-start | bytes 104 | tf_op jit(solution)/shard_map/ppermute | solution.py:414
  0.5 1.9 %collective-permute-start.26 = (s32[1]{0:T(128)}, s32[1]{0:T(128)}, u32[]{:S(2)}, u32[]{:S(2)}) collective-permute-start(s32[1]{0:T(128)} %param.16), channel_id=1, source_target_pairs={{0,8},{8,0},{32,40},{40,32},{64,72},{72,64},{96,104},{104,96},{128... | collective-permute-start | bytes 20 | tf_op jit(solution)/shard_map/ppermute | solution.py:414
  6.2 52.3 %copy-start.8 = (s32[16]{0:T(128)S(1)}, s32[16]{0:T(128)}, u32[]{:S(2)}) copy-start(s32[16]{0:T(128)} %get-tuple-element.113.rows_ref) | copy-start | bytes 196 | tf_op jit(solution)/shard_map/cond
  6.2 52.3 %copy-start.12 = (s32[8]{0:T(128)S(1)}, s32[8]{0:T(128)}, u32[]{:S(2)}) copy-start(s32[8]{0:T(128)} %get-tuple-element.114) | copy-start | bytes 100 | tf_op jit(solution)/shard_map/cond
  6.2 52.3 %copy-start.16 = (s32[8]{0:T(128)S(1)}, s32[8]{0:T(128)}, u32[]{:S(2)}) copy-start(s32[8]{0:T(128)} %get-tuple-element.115) | copy-start | bytes 100 | tf_op jit(solution)/shard_map/cond
  6.2 52.3 %all-to-all-start.2 = ((bf16[8,928,256]{2,1,0:T(8,128)(2,1)}), bf16[8,928,256]{2,1,0:T(8,128)(2,1)}, u32[]{:S(2)}, u32[]{:S(2)}) async-start(bf16[8,928,256]{2,1,0:T(8,128)(2,1)} %broadcast_in_dim.10), calls=%async_computation.2 | async-start | bytes 7602176 | tf_op jit(solution)/shard_map/cond/branch_2_fun/all_to_all | solution.py:391
  13.7 46.2 %collective-permute-start.14 = (bf16[8,512,512]{2,1,0:T(8,128)(2,1)}, bf16[8,512,512]{2,1,0:T(8,128)(2,1)}, u32[]{:S(2)}, u32[]{:S(2)}) collective-permute-start(bf16[8,512,512]{2,1,0:T(8,128)(2,1)} %get-tuple-element.122.near_right), channel_id=1, source_target_pairs={{0,8},{8,0},{32,40},{40,32},{64,72},{72,64},{96,104},{104,96},{128... | collective-permute-start | bytes 12582920 | tf_op jit(solution)/shard_map/cond/branch_2_fun/ppermute | solution.py:390
  13.7 46.2 %collective-permute-start.13 = (bf16[8,512,512]{2,1,0:T(8,128)(2,1)}, bf16[8,512,512]{2,1,0:T(8,128)(2,1)}, u32[]{:S(2)}, u32[]{:S(2)}) collective-permute-start(bf16[8,512,512]{2,1,0:T(8,128)(2,1)} %get-tuple-element.121), channel_id=1, source_target_pairs={{0,8},{8,0},{32,40},{40,32},{64,72},{72,64},{96,104},{104,96},{128... | collective-permute-start | bytes 12582920 | tf_op jit(solution)/shard_map/cond/branch_2_fun/ppermute | solution.py:389
  58.5 6.9 %collective-permute-start.12 = (bf16[7424,256]{1,0:T(8,128)(2,1)}, bf16[7424,256]{1,0:T(8,128)(2,1)}, u32[]{:S(2)}, u32[]{:S(2)}) collective-permute-start(bf16[7424,256]{1,0:T(8,128)(2,1)} %bitcast.6.near_wave), channel_id=1, source_target_pairs={{0,8},{8,0},{32,40},{40,32},{64,72},{72,64},{96,104},{104,96},{128... | collective-permute-start | bytes 11403272 | tf_op jit(solution)/shard_map/cond/branch_2_fun/ppermute | solution.py:392
  65.4 10.0 %copy-start.2 = (bf16[8,512,512]{2,1,0:T(8,128)(2,1)S(1)}, bf16[8,512,512]{2,1,0:T(8,128)(2,1)}, u32[]{:S(2)}) copy-start(bf16[8,512,512]{2,1,0:T(8,128)(2,1)} %get-tuple-element.121) | copy-start | bytes 12582916 | tf_op jit(solution)/shard_map/cond
  73.2 13.7 %collective-permute-start.15 = (bf16[768,512]{1,0:T(8,128)(2,1)S(1)}, bf16[768,512]{1,0:T(8,128)(2,1)S(1)}, u32[]{:S(2)}, u32[]{:S(2)}) collective-permute-start(bf16[768,512]{1,0:T(8,128)(2,1)S(1)} %get-tuple-element.124), channel_id=1, source_target_pairs={{0,4},{8,9},{32,36},{40,41},{64,68},{72,73},{96,100},{104,105},{12... | collective-permute-start | bytes 2359304 | tf_op jit(solution)/shard_map/cond/branch_2_fun/ppermute | solution.py:397
  75.4 19.9 %collective-permute-start.16 = (bf16[768,512]{1,0:T(8,128)(2,1)S(1)}, bf16[768,512]{1,0:T(8,128)(2,1)S(1)}, u32[]{:S(2)}, u32[]{:S(2)}) collective-permute-start(bf16[768,512]{1,0:T(8,128)(2,1)S(1)} %get-tuple-element.125), channel_id=1, source_target_pairs={{0,2},{8,25},{32,34},{40,57},{64,66},{72,89},{96,98},{104,121},{12... | collective-permute-start | bytes 2359304 | tf_op jit(solution)/shard_map/cond/branch_2_fun/ppermute | solution.py:397
  84.6 12.1 %collective-permute-start.17 = (bf16[768,512]{1,0:T(8,128)(2,1)S(1)}, bf16[768,512]{1,0:T(8,128)(2,1)S(1)}, u32[]{:S(2)}, u32[]{:S(2)}) collective-permute-start(bf16[768,512]{1,0:T(8,128)(2,1)S(1)} %get-tuple-element.126), channel_id=1, source_target_pairs={{0,6},{8,24},{32,38},{40,56},{64,70},{72,88},{96,102},{104,120},{1... | collective-permute-start | bytes 2359304 | tf_op jit(solution)/shard_map/cond/branch_2_fun/ppermute | solution.py:399
  99.1 6.6 %collective-permute-start.27 = (bf16[256,512]{1,0:T(8,128)(2,1)}, bf16[256,512]{1,0:T(8,128)(2,1)S(1)}, u32[]{:S(2)}, u32[]{:S(2)}) collective-permute-start(bf16[256,512]{1,0:T(8,128)(2,1)} %get-tuple-element.146), channel_id=1, source_target_pairs={{0,16},{8,10},{32,48},{40,42},{64,80},{72,74},{96,112},{104,106},{... | collective-permute-start | bytes 786440 | tf_op jit(solution)/shard_map/ppermute | solution.py:417
  100.3 8.1 %collective-permute-start.28 = (bf16[256,512]{1,0:T(8,128)(2,1)}, bf16[256,512]{1,0:T(8,128)(2,1)S(1)}, u32[]{:S(2)}, u32[]{:S(2)}) collective-permute-start(bf16[256,512]{1,0:T(8,128)(2,1)} %get-tuple-element.147), channel_id=1, source_target_pairs={{0,1},{8,12},{32,33},{40,44},{64,65},{72,76},{96,97},{104,108},{12... | collective-permute-start | bytes 786440 | tf_op jit(solution)/shard_map/ppermute | solution.py:417
  102.9 8.2 %collective-permute-start.29 = (bf16[256,512]{1,0:T(8,128)(2,1)}, bf16[256,512]{1,0:T(8,128)(2,1)S(1)}, u32[]{:S(2)}, u32[]{:S(2)}) collective-permute-start(bf16[256,512]{1,0:T(8,128)(2,1)} %get-tuple-element.148), channel_id=1, source_target_pairs={{0,17},{8,14},{32,49},{40,46},{64,81},{72,78},{96,113},{104,110},{... | collective-permute-start | bytes 786440 | tf_op jit(solution)/shard_map/ppermute | solution.py:417
  105.7 5.5 %copy-start.3 = (bf16[256,512]{1,0:T(8,128)(2,1)}, bf16[256,512]{1,0:T(8,128)(2,1)S(1)}, u32[]{:S(2)}) copy-start(bf16[256,512]{1,0:T(8,128)(2,1)S(1)} %collective-permute-done.27.got1) | copy-start | bytes 786436
  108.4 2.8 %copy-start.4 = (bf16[256,512]{1,0:T(8,128)(2,1)}, bf16[256,512]{1,0:T(8,128)(2,1)S(1)}, u32[]{:S(2)}) copy-start(bf16[256,512]{1,0:T(8,128)(2,1)S(1)} %collective-permute-done.28.got2) | copy-start | bytes 786436
  111.2 0.7 copy-start.5
